TPU v7x, 32 devices: a whole 2x2x4 slice. The times are simulated.
32 devices in a mesh: section: 2 (over x), row: 4 (over z), col: 4 (over y, core).
Axes of the slice: x: 2, y: 2, z: 4, core: 2. Of those that a mesh axis runs over, the one named last changes fastest.
Arguments:
- grad_top: bfloat16 [1024, 12288], P(None, 'row'), may hold values from -6 to 6
- qkv_grad: bfloat16 [2, 1024, 18432], P('section', 'col', 'row'), may hold values from -1.5 to 1.5
- qkv_input: bfloat16 [2, 1024, 12288], P('section', None, 'row'), may hold values from -6 to 6
- qkv_weight: bfloat16 [2, 12288, 18432], P('section', 'row', 'col'), may hold values from -0.0546875 to 0.0546875
- attn_out: bfloat16 [2, 1024, 6144], P('section', None, 'col'), may hold values from -1.5 to 1.5
- out_weight: bfloat16 [2, 6144, 12288], P('section', 'col', 'row'), may hold values from -0.078125 to 0.078125
Outputs:
- qkv_weight_grad: bfloat16 [2, 12288, 18432], P('section', 'row', 'col')
- out_weight_grad: bfloat16 [2, 6144, 12288], P('section', 'col', 'row')
- attn_grad: bfloat16 [2, 1024, 6144], P('section', 'row', 'col')
- lower_grad: bfloat16 [2, 1024, 12288], P('section', 'col', 'row')
All inputs are finite; a program needn't handle non-finite values.
Results may differ from a plain program's by a relative error of at most 0.014.
Values may be sent and summed in bfloat16 or wider, within the bound.
No kernel may reach another device: no remote copies, remote signals or barrier semaphores. Data moves between devices by JAX's collectives and lax.ppermute only.
A program may use at most 192 MiB of HBM per device.

v0:
```python
import jax
import jax.numpy as jnp
from jax import lax
from jax.sharding import PartitionSpec as P


def broadcast(value, axis, source):
    kept = jnp.where(lax.axis_index(axis) == source, value, 0).astype(value.dtype)
    return lax.psum(kept, axis)


def shifted(block, axis, distance):
    devices = range(lax.axis_size(axis))
    route = [(i - distance, i) for i in devices if i - distance in devices]
    return lax.ppermute(block, axis, route)


def contract_rows(left_side, right_side):
    return lax.dot_general(
        left_side, right_side, (((0,), (0,)), ((), ())), preferred_element_type=jnp.float32
    )


def contract_cols(left_side, right_side):
    return lax.dot_general(
        left_side, right_side, (((1,), (1,)), ((), ())), preferred_element_type=jnp.float32
    )


def per_device(grad_top, qkv_grad, qkv_input, qkv_weight, attn_out, out_weight):
    weight = qkv_weight[0]
    inputs = qkv_input[0]
    own_share = qkv_grad[0]
    token_count = inputs.shape[0]
    columns = lax.all_gather(own_share, "col", axis=0, tiled=True)
    turned = broadcast(columns, "row", lax.axis_index("col"))
    row_terms = contract_cols(turned, weight)
    grad_sum = contract_rows(inputs, turned)
    is_top = lax.axis_index("section") == lax.axis_size("section") - 1
    share_rows = token_count // lax.axis_size("col")
    share_first = lax.axis_index("col") * share_rows
    summed = lax.psum(row_terms.astype(jnp.bfloat16), "col").astype(jnp.float32)
    top_lower = (grad_top.astype(jnp.float32) + summed).astype(jnp.bfloat16)
    handed = shifted(top_lower, "section", -1)
    upper_grad = jnp.where(is_top, grad_top, handed)
    lower_full = (upper_grad.astype(jnp.float32) + summed).astype(jnp.bfloat16)
    lower_grad = lax.dynamic_slice_in_dim(lower_full, share_first, share_rows, 0)
    attn_rows = attn_out[0]
    out_tile = out_weight[0]
    out_grad = contract_rows(attn_rows, upper_grad)
    attn_grad = lax.psum_scatter(
        contract_cols(upper_grad, out_tile).astype(jnp.bfloat16),
        "row",
        scatter_dimension=0,
        tiled=True,
    )
    return (
        grad_sum.astype(jnp.bfloat16)[None],
        out_grad.astype(jnp.bfloat16)[None],
        attn_grad[None],
        lower_grad[None],
    )


def solution(mesh):
    return jax.shard_map(
        per_device,
        mesh=mesh,
        in_specs=(
            P(None, "row"),
            P("section", "col", "row"),
            P("section", None, "row"),
            P("section", "row", "col"),
            P("section", None, "col"),
            P("section", "col", "row"),
        ),
        out_specs=(
            P("section", "row", "col"),
            P("section", "col", "row"),
            P("section", "row", "col"),
            P("section", "col", "row"),
        ),
        check_vma=False,
    )
```

profile of v0, /device:TPU:0, one launch (start us, length us, event | category | flops | bytes accessed | tf_op | source)
XLA Modules:
  0.0 854.6 jit_solution(8101405396472301635)
XLA Ops:
  7.2 0.0 copy-start
  7.2 0.0 all-gather.3.cloned.1.call-start
  7.2 0.7 all-gather.3.cloned.1.call-update
  7.9 0.0 all-reduce.3.cloned.1.call-start
  8.0 68.6 %all-gather.3.cloned.1.call-done = bf16[1,1024,4608]{2,1,0:T(8,128)(2,1)} async-done(((bf16[1,256,4608]{2,1,0:T(8,128)(2,1)}), bf16[1,1024,4608]{2,1,0:T(8,128)(2,1)}) %all-gather.3.cloned.1.call-update) | async-done | bytes 9437200 | tf_op jit(solution)/shard_map/all_gather | solution.py:35
  76.5 8.0 select_bitcast_fusion
  84.6 0.0 all-reduce.3.cloned.1.call-update
  84.6 0.0 all-reduce.5.cloned.1.call-start
  84.7 324.7 %all-reduce.3.cloned.1.call-done = bf16[1024,4608]{1,0:T(8,128)(2,1)} async-done(((bf16[1024,4608]{1,0:T(8,128)(2,1)}), bf16[1024,4608]{1,0:T(8,128)(2,1)}) %all-reduce.3.cloned.1.call-update) | async-done | bytes 9437200 | tf_op jit(solution)/shard_map/psum | solution.py:9
  409.3 36.8 %fusion.7 = bf16[1024,3072]{1,0:T(8,128)(2,1)} fusion(bf16[1024,4608]{1,0:T(8,128)(2,1)} %all-reduce.3.cloned.1.call-done, bf16[1,3072,4608]{2,1,0:T(8,128)(2,1)} %param.9), kind=kOutput, calls=%fused_computation.12 | convolution fusion | flops 28994174976 | bytes 44040192 | tf_op jit(solution)/shard_map/dot_general | solution.py:25
  446.1 0.0 all-reduce.5.cloned.1.call-update
  446.2 0.0 reduce-scatter.2.cloned.1.call-start
  446.2 118.7 %all-reduce.5.cloned.1.call-done = bf16[1024,3072]{1,0:T(8,128)(2,1)} async-done(((bf16[1024,3072]{1,0:T(8,128)(2,1)}), bf16[1024,3072]{1,0:T(8,128)(2,1)}) %all-reduce.5.cloned.1.call-update) | async-done | bytes 6291472 | tf_op jit(solution)/shard_map/psum | solution.py:42
  564.9 10.1 %add_convert_fusion = bf16[1024,3072]{1,0:T(8,128)(2,1)} fusion(bf16[1024,3072]{1,0:T(8,128)(2,1)} %param.6, bf16[1024,3072]{1,0:T(8,128)(2,1)} %all-reduce.5.cloned.1.call-done), kind=kLoop, calls=%fused_computation.4 | loop fusion | flops 12582912 | bytes 18874368 | tf_op jit(solution)/shard_map/convert_element_type | solution.py:43
  575.0 1.3 collective-permute-start
  576.3 137.9 %collective-permute-done = bf16[1024,3072]{1,0:T(8,128)(2,1)} collective-permute-done((bf16[1024,3072]{1,0:T(8,128)(2,1)}, bf16[1024,3072]{1,0:T(8,128)(2,1)}, u32[]{:S(2)}, u32[]{:S(2)}) %collective-permute-start) | collective-permute-done | bytes 6291488 | tf_op jit(solution)/shard_map/ppermute | solution.py:15
  714.2 6.1 broadcast_select_fusion
  720.3 15.6 %fusion.10 = bf16[1024,1536]{1,0:T(8,128)(2,1)} fusion(bf16[1024,3072]{1,0:T(8,128)(2,1)} %broadcast_select_fusion, bf16[1,1536,3072]{2,1,0:T(8,128)(2,1)} %param.11), kind=kOutput, calls=%fused_computation.13 | convolution fusion | flops 9665249280 | bytes 18874368 | tf_op jit(solution)/shard_map/dot_general | solution.py:25
  735.9 0.0 reduce-scatter.2.cloned.1.call-update
  735.9 37.7 %fusion.2 = bf16[1,3072,4608]{1,2,0:T(8,128)(2,1)} fusion(bf16[1024,4608]{1,0:T(8,128)(2,1)} %all-reduce.3.cloned.1.call-done, bf16[1,1024,3072]{2,1,0:T(8,128)(2,1)} %param.8), kind=kOutput, calls=%fused_computation.3 | convolution fusion | flops 29005185024 | bytes 44040192 | tf_op jit(solution)/shard_map/dot_general | solution.py:19
  773.6 36.6 %copy.10 = bf16[1,3072,4608]{2,1,0:T(8,128)(2,1)} copy(bf16[1,3072,4608]{1,2,0:T(8,128)(2,1)} %fusion.2) | data formatting | bytes 56623104
  810.2 0.0 copy-start.1
  810.2 9.1 %convert_element_type.39 = f32[1024,3072]{1,0:T(8,128)} convert(bf16[1024,3072]{1,0:T(8,128)(2,1)} %all-reduce.5.cloned.1.call-done) | non-fusion elementwise | flops 3145728 | bytes 18874368 | tf_op jit(solution)/shard_map/convert_element_type | solution.py:42
  819.3 0.0 copy-done
  819.3 0.0 copy-done.1
  819.3 12.2 %fusion.3 = bf16[1,1536,3072]{1,2,0:T(8,128)(2,1)} fusion(bf16[1024,3072]{1,0:T(8,128)(2,1)S(1)} %copy-done.1, bf16[1,1024,1536]{2,1,0:T(8,128)(2,1)S(1)} %copy-done), kind=kOutput, calls=%fused_computation.6 | convolution fusion | flops 9668395008 | bytes 18874368 | tf_op jit(solution)/shard_map/dot_general | solution.py:19
  831.5 12.6 %copy.11 = bf16[1,1536,3072]{2,1,0:T(8,128)(2,1)} copy(bf16[1,1536,3072]{1,2,0:T(8,128)(2,1)} %fusion.3) | data formatting | bytes 18874368
  844.1 3.9 fusion.15
  848.0 0.0 reduce-scatter.2.cloned.1.call-done
Async XLA Ops:
  7.2 812.2 %copy-start = (bf16[1,1024,1536]{2,1,0:T(8,128)(2,1)S(1)}, bf16[1,1024,1536]{2,1,0:T(8,128)(2,1)}, u32[]{:S(2)}) copy-start(bf16[1,1024,1536]{2,1,0:T(8,128)(2,1)} %param.10) | copy-start | bytes 9437188
  7.2 69.4 %all-gather.3.cloned.1.call-start = ((), (), s32[]{:S(2)}) async-start(), calls=%async_computation.4 | async-start | bytes 11796480 | tf_op jit(solution)/shard_map/all_gather | solution.py:35
  7.9 401.4 %all-reduce.3.cloned.1.call-start = ((), (), s32[]{:S(2)}) async-start(), calls=%async_computation.1 | async-start | bytes 18874368 | tf_op jit(solution)/shard_map/psum | solution.py:9
  84.6 480.3 %all-reduce.5.cloned.1.call-start = ((), (), s32[]{:S(2)}) async-start(), calls=%async_computation.2 | async-start | bytes 12582912 | tf_op jit(solution)/shard_map/psum | solution.py:42
  446.2 401.9 %reduce-scatter.2.cloned.1.call-start = ((), (), s32[]{:S(2)}) async-start(), calls=%async_computation.3 | async-start | bytes 3932160 | tf_op jit(solution)/shard_map/reduce_scatter | solution.py:51
  575.0 139.2 %collective-permute-start = (bf16[1024,3072]{1,0:T(8,128)(2,1)}, bf16[1024,3072]{1,0:T(8,128)(2,1)}, u32[]{:S(2)}, u32[]{:S(2)}) collective-permute-start(bf16[1024,3072]{1,0:T(8,128)(2,1)} %add_convert_fusion), channel_id=1, source_target_pairs={{16,0},{17,1},{18,2},{19,3},{20,4},{21,5},{22,6},{23,7},{24,8},{25... | collective-permute-start | bytes 18874376 | tf_op jit(solution)/shard_map/ppermute | solution.py:15
  810.2 9.1 %copy-start.1 = (bf16[1024,3072]{1,0:T(8,128)(2,1)S(1)}, bf16[1024,3072]{1,0:T(8,128)(2,1)}, u32[]{:S(2)}) copy-start(bf16[1024,3072]{1,0:T(8,128)(2,1)} %broadcast_select_fusion) | copy-start | bytes 18874372
Sparse Core Ops, SparseCore 0:
  9.6 66.9 all-gather.2
  84.7 324.5 all-reduce.2
  446.3 118.5 all-reduce.4
  736.0 59.9 reduce-scatter.1
where the time goes:
time: 856 us; the launch traced here: 855 us
  waiting for transfers between devices  651 us (76%)
  matrix products  102 us (12%)
  local copies, waits for them, and re-layouts  49.2 us (6%)
  other arithmetic  37.3 us (4%)
  between operations  13.8 us (2%)
    psum x1, waiting for transfers between devices, broadcast(): return lax.psum(kept, axis)  325 us
    ppermute x1, waiting for transfers between devices, shifted(): return lax.ppermute(block, axis, route)  138 us
    psum x1, waiting for transfers between devices, per_device(): summed = lax.psum(row_terms.astype(jnp.bfloat16), 'col').astype(jnp.float32)  119 us
    all_gather x1, waiting for transfers between devices, per_device(): columns = lax.all_gather(own_share, 'col', axis=0, tiled=True)  68.6 us
    dot_general x2, matrix products, contract_cols(): lax.dot_general(left_side, right_side, (((1,), (1,)), ((), ())), preferre...  52.4 us
    dot_general x2, matrix products, contract_rows(): lax.dot_general(left_side, right_side, (((0,), (0,)), ((), ())), preferre...  49.9 us
    unnamed x6, local copies, waits for them, and re-layouts  49.2 us
  transfers between devices with their start and end apart: 5, of which 4 were waited for; matrix products, arithmetic and copies ran while one was open for 13% of the time, Pallas kernels for 0%

commit v1 on v0

v1 whole, which is shorter than its diff:
```python
import functools

import jax
import jax.numpy as jnp
from jax import lax
from jax.experimental import pallas as pl
from jax.experimental.pallas import tpu as pltpu
from jax.sharding import PartitionSpec as P

CHUNKS = (2, 1, 1)
PIECES = 3
VMEM = 60 * 2**20
BF16 = jnp.bfloat16
F32 = jnp.float32
EASE = 1
PARAMS = pltpu.CompilerParams(vmem_limit_bytes=VMEM)


def fitting(size, unit, most):
    return max(b for b in range(unit, most + 1, unit) if size % b == 0)


def cost(rows, depth, width):
    flops = 2 * rows * depth * width // EASE
    return pl.CostEstimate(flops=flops, bytes_accessed=flops // 1000, transcendentals=0)


def shape(dims, dtype):
    return jax.ShapeDtypeStruct(dims, dtype)


def swap(block, axis, bit):
    route = [(i, i ^ bit) for i in range(lax.axis_size(axis))]
    return lax.ppermute(block, axis, route)


def swap_below(block, bit):
    width = lax.axis_size("col")
    route = [
        (s * width + i, s * width + (i ^ bit))
        for s in range(lax.axis_size("section") - 1)
        for i in range(width)
    ]
    return lax.ppermute(block, ("section", "col"), route)


def shifted(block, axis, distance):
    devices = range(lax.axis_size(axis))
    route = [(i - distance, i) for i in devices if i - distance in devices]
    return lax.ppermute(block, axis, route)


def direct(block, step):
    n = lax.axis_size("row")
    route = [(j * n + (i ^ j ^ step), i * n + j) for i in range(n) for j in range(n)]
    return lax.ppermute(block, ("row", "col"), route)


def bits_down(n):
    return [1 << b for b in reversed(range(n.bit_length() - 1))]


def nt(left, right):
    return lax.dot_general(left, right, (((1,), (1,)), ((), ())), preferred_element_type=F32)


def turn_kernel(token, x_ref, out_ref):
    out_ref[...] = x_ref[...].T


def turned(token, x):
    n = token.shape[0]
    rows, cols = x.shape
    return pl.pallas_call(
        turn_kernel,
        out_shape=shape((cols, rows), x.dtype),
        grid_spec=pltpu.PrefetchScalarGridSpec(
            num_scalar_prefetch=1,
            grid=(n,),
            in_specs=[pl.BlockSpec((rows // n, cols), lambda d, token: (token[d], 0))],
            out_specs=pl.BlockSpec((cols, rows // n), lambda d, token: (0, d)),
        ),
        compiler_params=PARAMS,
        cost_estimate=cost(rows, cols, n),
        name="turn",
    )(token, x)


def halves(total, send_ref, keep_ref):
    for d in range(total.shape[0]):
        if d % 2:
            send_ref[d // 2] = total[d].astype(send_ref.dtype)
        else:
            keep_ref[d // 2] = total[d]


def terms_kernel(n, more, split, place, *refs):
    ins, weight_ref = refs[:n], refs[n]
    outs, held_ref = refs[n + 1 + more : -1], refs[-1]
    rows = ins[0].shape[0]

    @pl.when(pl.program_id(0) == 0)
    def _():
        for k in range(n):
            held_ref[pl.ds(pl.multiple_of(place[k] * rows, rows), rows), :] = ins[k][...]

    terms = nt(held_ref[...], weight_ref[...]).reshape(n, rows, -1)
    if more:
        terms = terms + refs[n + 1][...]
    if split:
        halves(terms, *outs)
    else:
        outs[0][...] = terms


def grad_terms(place, blocks, weight, piece, total=None, first=0, split=False):
    n = len(blocks)
    rows, depth = blocks[0].shape
    width = weight.shape[0]
    bn = fitting(width, 128, 512)
    more = total is not None
    chunk = first // rows
    keep = pl.BlockSpec((n // 2, rows, bn), lambda i, place: (0, 0, i))
    whole = pl.BlockSpec((n, rows, bn), lambda i, place: (0, 0, i))
    half = (n // 2, rows, width)
    sums = [shape(half, BF16), shape(half, F32)] if split else [shape((n, rows, width), F32)]
    return pl.pallas_call(
        functools.partial(terms_kernel, n, more, split),
        out_shape=sums + [shape((n * rows, depth), BF16)],
        grid_spec=pltpu.PrefetchScalarGridSpec(
            num_scalar_prefetch=1,
            grid=(width // bn,),
            in_specs=[pl.BlockSpec((rows, depth), lambda i, place: (0, 0))] * n
            + [pl.BlockSpec((bn, depth), lambda i, place: (i, piece))]
            + [pl.BlockSpec((n, rows, bn), lambda i, place: (0, chunk, i))] * more,
            out_specs=([keep, keep] if split else [whole])
            + [pl.BlockSpec((n * rows, depth), lambda i, place: (0, 0))],
        ),
        input_output_aliases={n + 2: 0} if more and not split else {},
        compiler_params=PARAMS,
        cost_estimate=cost(n * rows, depth, width),
        name="grad_terms",
    )(place, *blocks, weight, *[total] * more)


def attn_kernel(n, scalars, *refs):
    below, top = refs[:n], refs[n : 2 * n]
    weight_ref, send_ref, keep_ref, upper_ref, held_ref = refs[2 * n :]
    rows = below[0].shape[0]

    @pl.when(pl.program_id(0) == 0)
    def _():
        for d in range(n):
            upper = jnp.where(scalars[2 * n] == 1, top[d][0], below[d][...])
            upper_ref[d] = upper
            first = pl.multiple_of(scalars[n + d] * rows, rows)
            held_ref[pl.ds(first, rows), :] = upper

    terms = nt(held_ref[...], weight_ref[...])
    halves(terms.reshape(n, rows, -1), send_ref, keep_ref)


def attn_terms(scalars, below, grad_top, weight, first):
    n = len(below)
    rows, depth = below[0].shape
    width = weight.shape[0]
    bn = fitting(width, 128, 512)
    tops = grad_top.reshape(n, -1, depth)
    chunk = first // rows
    part = pl.BlockSpec((n // 2, rows, bn), lambda i, scalars: (0, 0, i))
    half = (n // 2, rows, width)
    return pl.pallas_call(
        functools.partial(attn_kernel, n),
        out_shape=[shape(half, BF16), shape(half, F32), shape((n, rows, depth), BF16)],
        grid_spec=pltpu.PrefetchScalarGridSpec(
            num_scalar_prefetch=1,
            grid=(width // bn,),
            in_specs=[pl.BlockSpec((rows, depth), lambda i, scalars: (0, 0))] * n
            + [
                pl.BlockSpec((1, rows, depth), lambda i, scalars, d=d: (scalars[d], chunk, 0))
                for d in range(n)
            ]
            + [pl.BlockSpec((bn, depth), lambda i, scalars: (i, 0))],
            out_specs=[
                part,
                part,
                pl.BlockSpec((n, rows, depth), lambda i, scalars: (0, 0, 0)),
            ],
            scratch_shapes=[pltpu.VMEM((n * rows, depth), BF16)],
        ),
        compiler_params=PARAMS,
        cost_estimate=cost(n * rows, depth, width),
        name="attn_terms",
    )(scalars, *below, *[tops] * n, weight)


def outer_kernel(order, scalars, left_ref, *refs):
    ins, out_ref = refs[: len(refs) - 1], refs[-1]
    right = [ins[a][first : first + rows] for a, first, rows in order]
    right = jnp.concatenate(right, axis=0) if len(right) > 1 else right[0]
    out_ref[...] = jnp.dot(left_ref[...], right, preferred_element_type=F32).astype(out_ref.dtype)


def outer_into_kernel(order, scalars, into_ref, left_ref, *refs):
    outer_kernel(order, scalars, left_ref, *refs)


def outer(scalars, left, rights, order, columns, first=0, into=None, part=(0, 1)):
    width = rights[0].shape[1] // part[1]
    bn = fitting(width, 128, 256)
    start = part[0] * width // bn
    offset = first // bn + start
    in_specs = [pl.BlockSpec(left.shape, lambda i, s: (0, 0))] + [
        pl.BlockSpec((a.shape[0], bn), lambda i, s: (0, i + start)) for a in rights
    ]
    kernel, args, aliases = outer_kernel, (left, *rights), {}
    if into is not None:
        in_specs = [pl.BlockSpec(memory_space=pl.ANY)] + in_specs
        kernel, args, aliases = outer_into_kernel, (into, *args), {1: 0}
    return pl.pallas_call(
        functools.partial(kernel, order),
        out_shape=shape((left.shape[0], columns), BF16),
        grid_spec=pltpu.PrefetchScalarGridSpec(
            num_scalar_prefetch=1,
            grid=(width // bn,),
            in_specs=in_specs,
            out_specs=pl.BlockSpec((left.shape[0], bn), lambda i, s: (0, i + offset)),
        ),
        input_output_aliases=aliases,
        compiler_params=PARAMS,
        cost_estimate=cost(*left.shape, width),
        name="outer",
    )(scalars, *args)


class Slots:
    def __init__(self):
        self.token = ()
        self.tasks = []

    def gate(self, block):
        return lax.optimization_barrier((block, self.token))[0]

    def run(self, choose):
        before, behind, tasks = [], [], []
        for task in self.tasks:
            step = next(task, None)
            if step is not None:
                before += step[0]
                behind += step[1]
                tasks.append(task)
        self.tasks = tasks
        token = self.token
        self.token = (*token, *before)
        for kernel in choose():
            made = kernel()
            behind.append(made)
            self.token = (made,)
        self.token = tuple(behind) or token


def summed(terms):
    total = terms[0].astype(F32)
    for term in terms[1:]:
        total = total + term.astype(F32)
    return total


def scatter(slots, send, keep, axis, short, done):
    terms = [[keep[p]] for p in range(keep.shape[0])]
    bit = 1
    before = []
    while True:
        got = swap(slots.gate(send), axis, bit)
        if bit > 1 or not short:
            yield before, [got]
            got = slots.gate(got)
        terms = [t + [got[p]] for p, t in enumerate(terms)]
        bit *= 2
        if bit == lax.axis_size(axis):
            break
        send = jnp.stack([summed(t) for t in terms[1::2]]).astype(BF16)
        before = [send]
        terms = terms[0::2]
    done += terms[0]


def per_device(grad_top, qkv_grad, qkv_input, qkv_weight, attn_out, out_weight):
    weight, own, out_tile = qkv_weight[0], qkv_grad[0], out_weight[0]
    n = lax.axis_size("row")
    row, col = lax.axis_index("row"), lax.axis_index("col")
    is_top = lax.axis_index("section") == lax.axis_size("section") - 1
    steps = jnp.arange(n, dtype=jnp.int32)
    token = col ^ steps
    share, columns = own.shape
    width = columns // PIECES
    unit = share // sum(CHUNKS)
    spans = [(sum(CHUNKS[:q]) * unit, c * unit) for q, c in enumerate(CHUNKS)]
    order = [(q, d * rows, rows) for d in range(n) for q, (_, rows) in enumerate(spans)]
    last_piece = PIECES - 1

    place = row ^ steps
    scalars = jnp.concatenate([token, row ^ col ^ steps, is_top.astype(jnp.int32)[None]])
    slots = Slots()
    have = {}

    def gather():
        for piece in range(PIECES):
            for q, (first, rows) in enumerate(spans if piece == last_piece else [(0, share)]):
                part = own[first : first + rows, piece * width : (piece + 1) * width]
                part = slots.gate(part)
                blocks = [direct(part, k) for k in range(n)]
                yield [], blocks
                have["blocks", piece, q] = blocks

    def relay(q):
        first, rows = spans[q]
        send, keep = have["terms", q]
        terms = []
        yield from scatter(slots, send, keep, "col", True, terms)
        down = summed(terms)
        top_own = lax.dynamic_slice_in_dim(grad_top, col * share + first, rows, 0)
        upper = top_own
        lower = (upper.astype(F32) + down).astype(BF16)
        for _ in range(lax.axis_size("section") - 1):
            handed = shifted(slots.gate(lower), "section", -1)
            yield [lower], [handed]
            handed = slots.gate(handed)
            upper = jnp.where(is_top, top_own, handed)
            lower = (upper.astype(F32) + down).astype(BF16)
        below = {0: handed}
        for bit in bits_down(n):
            got = {d | bit: swap_below(below[d], bit) for d in below}
            if bit > 1:
                yield [], list(got.values())
                got = {d: slots.gate(block) for d, block in got.items()}
                have["lower", q] = (slots.gate(upper).astype(F32) + down).astype(BF16)
            below.update(got)
        have["upper", q] = [below[d] for d in range(n)]

    def finish(q):
        send, keep = have["attn terms", q]
        terms = []
        yield from scatter(slots, send, keep, "row", False, terms)
        have["attn", q] = summed(terms).astype(BF16)

    def turn(name, array):
        def run():
            have[name] = turned(slots.gate(token), array)
            return have[name]

        return run

    def early_terms(piece):
        def run():
            have["early"], have["held", piece] = grad_terms(
                slots.gate(place), have["blocks", piece, 0], weight, piece, have.get("early")
            )
            return have["early"]

        return run

    def early_grad(piece):
        def run():
            have["grad"] = outer(
                slots.gate(place),
                have["inputs"],
                [have["held", piece]],
                [(0, 0, n * share)],
                columns,
                piece * width,
                have.get("grad"),
            )
            return have["grad"]

        return run

    def late_terms(q):
        def run():
            send, keep, have["late", q] = grad_terms(
                slots.gate(place),
                have["blocks", last_piece, q],
                weight,
                last_piece,
                have["early"],
                spans[q][0],
                True,
            )
            have["terms", q] = send, keep
            slots.tasks.append(relay(q))
            return send

        return run

    def late_grad(*part):
        def run():
            have["grad"] = outer(
                slots.gate(place),
                have["inputs"],
                [have["late", q] for q in range(len(spans))],
                order,
                columns,
                last_piece * width,
                have["grad"],
                part,
            )
            return have["grad"]

        return run

    def attn(q):
        def run():
            send, keep, upper = attn_terms(
                slots.gate(scalars), have["upper", q], grad_top, out_tile, spans[q][0]
            )
            have["attn terms", q] = send, keep
            have["uppers", q] = upper.reshape(-1, upper.shape[-1])
            slots.tasks.append(finish(q))
            return send

        return run

    def out_grad(*part):
        def run():
            have["out"] = outer(
                slots.gate(place),
                have["attn_out"],
                [have["uppers", q] for q in range(len(spans))],
                order,
                grad_top.shape[1],
                0,
                have.get("out"),
                part,
            )
            return have["out"]

        return run

    terms = [late_terms(q) for q in range(len(spans))]
    attns = [attn(q) for q in range(len(spans))]
    spare = [early_grad(last_piece - 1), late_grad(0, 2), late_grad(1, 2)]
    outs = [out_grad(0, 2), out_grad(1, 2)]

    def late():
        if terms:
            return [terms.pop(0)]
        if attns and ("upper", len(spans) - len(attns)) in have:
            more = len(attns) < len(spans) and len(attns) > 1
            return [attns.pop(0)] + [spare.pop(0) for _ in spare[: int(more)]]
        if spare and attns:
            return [spare.pop(0)]
        return [kernel for few in (spare, outs) for kernel in [few.pop(0) for _ in few[:1]]]

    slots.tasks.append(gather())
    slots.run(lambda: [turn("inputs", qkv_input[0]), turn("attn_out", attn_out[0])])
    for piece in range(last_piece):
        both = piece < last_piece - 1
        slots.run(lambda: [early_terms(piece)] + [early_grad(piece)] * both)
    while slots.tasks or terms or attns or spare or outs:
        slots.run(late)

    every = range(len(spans))
    return (
        have["grad"][None],
        have["out"][None],
        jnp.concatenate([have["attn", q] for q in every], axis=0)[None],
        jnp.concatenate([have["lower", q] for q in every], axis=0)[None],
    )


def solution(mesh):
    return jax.shard_map(
        per_device,
        mesh=mesh,
        in_specs=(
            P(None, "row"),
            P("section", "col", "row"),
            P("section", None, "row"),
            P("section", "row", "col"),
            P("section", None, "col"),
            P("section", "col", "row"),
        ),
        out_specs=(
            P("section", "row", "col"),
            P("section", "col", "row"),
            P("section", "row", "col"),
            P("section", "col", "row"),
        ),
        check_vma=False,
    )
```

time: 856 us -> 455 us (0.53)
  waiting for transfers between devices: 651 us -> 53 us
  Pallas kernels: 0 us -> 183 us
  starting transfers between devices: 1.44 us -> 178 us
  matrix products: 102 us -> 0 us
  local copies, waits for them, and re-layouts: 49.2 us -> 6.04 us
  between operations: 13.8 us -> 1.43 us
    psum x2 -> x0, waiting for transfers between devices: 443 us -> none  [the longest x1 325 us: broadcast(): return lax.psum(kept, axis)]
    pallas_call x0 -> x16, Pallas kernels: none -> 183 us  [the longest x6 73.5 us: outer(): pl.pallas_call(functools.partial(kernel, order), out_shape=shape((left.sh...]
    ppermute x0 -> x41, starting transfers between devices: none -> 173 us  [the longest x20 139 us: direct(): return lax.ppermute(block, ('row', 'col'), route)]
    ppermute x1 -> x3, waiting for transfers between devices: 138 us -> 5.92 us  [shifted(): return lax.ppermute(block, axis, route)]
    dot_general x4 -> x0, matrix products: 102 us -> none  [the longest x2 52.4 us: contract_cols(): lax.dot_general(left_side, right_side, (((1,), (1,)), ((), ())), preferre...]
    all_gather x1 -> x0, waiting for transfers between devices: 68.6 us -> none  [per_device(): columns = lax.all_gather(own_share, 'col', axis=0, tiled=True)]
    unnamed x6 -> x74, local copies, waits for them, and re-layouts: 49.2 us -> 1.02 us
    ppermute x0 -> x41, waiting for transfers between devices: none -> 47.1 us  [the longest x20 32.1 us: direct(): return lax.ppermute(block, ('row', 'col'), route)]
  transfers between devices with their start and end apart: 5 -> 44, of which waited for: 4 -> 10; matrix products, arithmetic and copies ran while one was open for 13% -> 6% of each run, Pallas kernels for 0% -> 38%
where the time goes in v1:
time: 455 us; the launch traced here: 453 us
  Pallas kernels  183 us (40%)
  starting transfers between devices  178 us (39%)
  waiting for transfers between devices  53 us (12%)
  other arithmetic  31.3 us (7%)
  local copies, waits for them, and re-layouts  6.04 us (1%)
    ppermute x20, starting transfers between devices, direct(): return lax.ppermute(block, ('row', 'col'), route)  139 us
    pallas_call x6, Pallas kernels, outer(): pl.pallas_call(functools.partial(kernel, order), out_shape=shape((left.sh...  73.5 us
    pallas_call x5, Pallas kernels, grad_terms(): pl.pallas_call(functools.partial(terms_kernel, n, more, split), out_shape...  67.4 us
    ppermute x20, waiting for transfers between devices, direct(): return lax.ppermute(block, ('row', 'col'), route)  32.1 us
    pallas_call x3, Pallas kernels, attn_terms(): pl.pallas_call(functools.partial(attn_kernel, n), out_shape=[shape(half,...  30 us
    ppermute x9, starting transfers between devices, swap_below(): return lax.ppermute(block, ('section', 'col'), route)  23.7 us
    ppermute x12, waiting for transfers between devices, swap(): return lax.ppermute(block, axis, route)  14.9 us
    pallas_call x2, Pallas kernels, turned(): pl.pallas_call(turn_kernel, out_shape=shape((cols, rows), x.dtype), grid_...  12.6 us
  transfers between devices with their start and end apart: 44, of which 10 were waited for; matrix products, arithmetic and copies ran while one was open for 6% of the time, Pallas kernels for 38%

profile of v1, /device:TPU:0, one launch (start us, length us, event | category | flops | bytes accessed | tf_op | source)
XLA Modules:
  0.0 452.8 jit_solution(13722033120220949423)
XLA Ops:
  2.8 6.1 %collective-permute-start.1 = (bf16[256,1536]{1,0:T(8,128)(2,1)S(1)}, bf16[256,1536]{1,0:T(8,128)(2,1)S(1)}, u32[]{:S(2)}, u32[]{:S(2)}) collective-permute-start(bf16[256,1536]{1,0:T(8,128)(2,1)S(1)} %get-tuple-element.156), channel_id=1, source_target_pairs={{1,0},{4,1},{11,2},{14,3},{0,4},{5,5},{10,6},{15,7},{3,8},{6,9},{9... | collective-permute-start | bytes 2359304 | tf_op jit(solution)/shard_map/ppermute | solution.py:56
  9.0 5.5 %collective-permute-start.2 = (bf16[256,1536]{1,0:T(8,128)(2,1)S(1)}, bf16[256,1536]{1,0:T(8,128)(2,1)}, u32[]{:S(2)}, u32[]{:S(2)}) collective-permute-start(bf16[256,1536]{1,0:T(8,128)(2,1)S(1)} %get-tuple-element.156), channel_id=1, source_target_pairs={{2,0},{7,1},{8,2},{13,3},{3,4},{6,5},{9,6},{12,7},{0,8},{5,9},{10,... | collective-permute-start | bytes 2359304 | tf_op jit(solution)/shard_map/ppermute | solution.py:56
  14.4 4.5 collective-permute-start.3
  21.2 7.2 %turn.2.left_ref = bf16[3072,1024]{1,0:T(8,128)(2,1)} custom-call(s32[4]{0:T(128)} %iota_xor_fusion.1.token, bf16[1024,3072]{1,0:T(8,128)(2,1)} %bitcast.67), custom_call_target="tpu_custom_call" | custom-call | flops 25165824 | bytes 25165 | tf_op jit(solution)/shard_map/turn/pallas_call | solution.py:74
  28.4 5.4 %turn.3.left_ref = bf16[1536,1024]{1,0:T(8,128)(2,1)} custom-call(s32[4]{0:T(128)} %iota_xor_fusion.1.token, bf16[1024,1536]{1,0:T(8,128)(2,1)} %bitcast.72), custom_call_target="tpu_custom_call" | custom-call | flops 12582912 | bytes 12582 | tf_op jit(solution)/shard_map/turn/pallas_call | solution.py:74
  36.2 12.5 %collective-permute-done.2.refs_2_ = bf16[256,1536]{1,0:T(8,128)(2,1)} collective-permute-done((bf16[256,1536]{1,0:T(8,128)(2,1)S(1)}, bf16[256,1536]{1,0:T(8,128)(2,1)}, u32[]{:S(2)}, u32[]{:S(2)}) %collective-permute-start.2) | collective-permute-done | bytes 786464 | tf_op jit(solution)/shard_map/ppermute | solution.py:56
  48.7 9.4 %collective-permute-done.3.refs_3_ = bf16[256,1536]{1,0:T(8,128)(2,1)} collective-permute-done((bf16[256,1536]{1,0:T(8,128)(2,1)S(1)}, bf16[256,1536]{1,0:T(8,128)(2,1)}, u32[]{:S(2)}, u32[]{:S(2)}) %collective-permute-start.3) | collective-permute-done | bytes 786464 | tf_op jit(solution)/shard_map/ppermute | solution.py:56
  58.9 27.7 %collective-permute-start.5 = (bf16[256,1536]{1,0:T(8,128)(2,1)S(1)}, bf16[256,1536]{1,0:T(8,128)(2,1)S(1)}, u32[]{:S(2)}, u32[]{:S(2)}) collective-permute-start(bf16[256,1536]{1,0:T(8,128)(2,1)S(1)} %get-tuple-element.79), channel_id=1, source_target_pairs={{1,0},{4,1},{11,2},{14,3},{0,4},{5,5},{10,6},{15,7},{3,8},{6,9},{9... | collective-permute-start | bytes 2359304 | tf_op jit(solution)/shard_map/ppermute | solution.py:56
  86.6 5.6 %collective-permute-start.6 = (bf16[256,1536]{1,0:T(8,128)(2,1)S(1)}, bf16[256,1536]{1,0:T(8,128)(2,1)S(1)}, u32[]{:S(2)}, u32[]{:S(2)}) collective-permute-start(bf16[256,1536]{1,0:T(8,128)(2,1)S(1)} %get-tuple-element.79), channel_id=1, source_target_pairs={{2,0},{7,1},{8,2},{13,3},{3,4},{6,5},{9,6},{12,7},{0,8},{5,9},{10,... | collective-permute-start | bytes 2359304 | tf_op jit(solution)/shard_map/ppermute | solution.py:56
  92.1 5.7 %collective-permute-start.7 = (bf16[256,1536]{1,0:T(8,128)(2,1)S(1)}, bf16[256,1536]{1,0:T(8,128)(2,1)}, u32[]{:S(2)}, u32[]{:S(2)}) collective-permute-start(bf16[256,1536]{1,0:T(8,128)(2,1)S(1)} %get-tuple-element.79), channel_id=1, source_target_pairs={{3,0},{6,1},{9,2},{12,3},{2,4},{7,5},{8,6},{13,7},{1,8},{4,9},{11,... | collective-permute-start | bytes 2359304 | tf_op jit(solution)/shard_map/ppermute | solution.py:56
  97.9 16.9 %grad_terms.5 = (f32[4,256,3072]{2,1,0:T(8,128)}, bf16[1024,1536]{1,0:T(8,128)(2,1)}) custom-call(s32[4]{0:T(128)} %iota_xor_fusion.2.place.scalars, bf16[256,1536]{1,0:T(8,128)(2,1)} %copy-done.34, bf16[256,1536]{1,0:T(8,128)(2,1)} %copy-done.35, bf16[256,1536]{1,0:T(8,128)(2,1)} %collective-permute-done.2.refs_2_, ...), custom_call_target="tpu_custom_call" | custom-call | flops 9663676416 | bytes 9663676 | tf_op jit(solution)/shard_map/grad_terms/pallas_call | solution.py:127
  114.7 15.7 %outer.6.into_ref = bf16[3072,4608]{1,0:T(8,128)(2,1)} custom-call(s32[4]{0:T(128)} %iota_xor_fusion.2.place.scalars, bf16[3072,1024]{1,0:T(8,128)(2,1)} %turn.2.left_ref, bf16[1024,1536]{1,0:T(8,128)(2,1)} %get-tuple-element.83.refs_0_), custom_call_target="tpu_custom_call" | custom-call | flops 9663676416 | bytes 9663676 | tf_op jit(solution)/shard_map/outer/pallas_call | solution.py:220
  130.5 5.1 %collective-permute-done.7.refs_3_ = bf16[256,1536]{1,0:T(8,128)(2,1)} collective-permute-done((bf16[256,1536]{1,0:T(8,128)(2,1)S(1)}, bf16[256,1536]{1,0:T(8,128)(2,1)}, u32[]{:S(2)}, u32[]{:S(2)}) %collective-permute-start.7) | collective-permute-done | bytes 786464 | tf_op jit(solution)/shard_map/ppermute | solution.py:56
  135.6 33.5 %collective-permute-start.10 = (bf16[128,1536]{1,0:T(8,128)(2,1)}, bf16[128,1536]{1,0:T(8,128)(2,1)S(1)}, u32[]{:S(2)}, u32[]{:S(2)}) collective-permute-start(bf16[128,1536]{1,0:T(8,128)(2,1)} %slice.116), channel_id=1, source_target_pairs={{2,0},{7,1},{8,2},{13,3},{3,4},{6,5},{9,6},{12,7},{0,8},{5,9},{10,... | collective-permute-start | bytes 1179656 | tf_op jit(solution)/shard_map/ppermute | solution.py:56
  172.7 5.9 %collective-permute-start.9 = (bf16[128,1536]{1,0:T(8,128)(2,1)}, bf16[128,1536]{1,0:T(8,128)(2,1)S(1)}, u32[]{:S(2)}, u32[]{:S(2)}) collective-permute-start(bf16[128,1536]{1,0:T(8,128)(2,1)} %slice.116), channel_id=1, source_target_pairs={{1,0},{4,1},{11,2},{14,3},{0,4},{5,5},{10,6},{15,7},{3,8},{6,9},{9... | collective-permute-start | bytes 1179656 | tf_op jit(solution)/shard_map/ppermute | solution.py:56
  178.7 19.1 %grad_terms.6 = (f32[4,256,3072]{2,1,0:T(8,128)}, bf16[1024,1536]{1,0:T(8,128)(2,1)}) custom-call(s32[4]{0:T(128)} %iota_xor_fusion.2.place.scalars, bf16[256,1536]{1,0:T(8,128)(2,1)} %copy-done.20, bf16[256,1536]{1,0:T(8,128)(2,1)} %copy-done.21, bf16[256,1536]{1,0:T(8,128)(2,1)} %copy-done.22, ...), custom_call_target="tpu_custom_call", output_to_operand_aliasing={{0}: (6, {})} | custom-call | flops 9663676416 | bytes 9663676 | tf_op jit(solution)/shard_map/grad_terms/pallas_call | solution.py:127
  199.5 4.7 %collective-permute-start.13 = (bf16[64,1536]{1,0:T(8,128)(2,1)}, bf16[64,1536]{1,0:T(8,128)(2,1)S(1)}, u32[]{:S(2)}, u32[]{:S(2)}) collective-permute-start(bf16[64,1536]{1,0:T(8,128)(2,1)} %get-tuple-element.90), channel_id=1, source_target_pairs={{1,0},{4,1},{11,2},{14,3},{0,4},{5,5},{10,6},{15,7},{3,8},{6,9},{9... | collective-permute-start | bytes 589832 | tf_op jit(solution)/shard_map/ppermute | solution.py:56
  204.2 16.4 %collective-permute-start.14 = (bf16[64,1536]{1,0:T(8,128)(2,1)}, bf16[64,1536]{1,0:T(8,128)(2,1)S(1)}, u32[]{:S(2)}, u32[]{:S(2)}) collective-permute-start(bf16[64,1536]{1,0:T(8,128)(2,1)} %get-tuple-element.90), channel_id=1, source_target_pairs={{2,0},{7,1},{8,2},{13,3},{3,4},{6,5},{9,6},{12,7},{0,8},{5,9},{10,... | collective-permute-start | bytes 589832 | tf_op jit(solution)/shard_map/ppermute | solution.py:56
  220.6 5.0 %collective-permute-start.15 = (bf16[64,1536]{1,0:T(8,128)(2,1)}, bf16[64,1536]{1,0:T(8,128)(2,1)S(1)}, u32[]{:S(2)}, u32[]{:S(2)}) collective-permute-start(bf16[64,1536]{1,0:T(8,128)(2,1)} %get-tuple-element.90), channel_id=1, source_target_pairs={{3,0},{6,1},{9,2},{12,3},{2,4},{7,5},{8,6},{13,7},{1,8},{4,9},{11,... | collective-permute-start | bytes 589832 | tf_op jit(solution)/shard_map/ppermute | solution.py:56
  225.6 12.4 %grad_terms.7 = (bf16[2,128,3072]{2,1,0:T(8,128)(2,1)}, f32[2,128,3072]{2,1,0:T(8,128)}, bf16[512,1536]{1,0:T(8,128)(2,1)}) custom-call(s32[4]{0:T(128)} %iota_xor_fusion.2.place.scalars, bf16[128,1536]{1,0:T(8,128)(2,1)} %copy-done.25, bf16[128,1536]{1,0:T(8,128)(2,1)} %copy-done.26, bf16[128,1536]{1,0:T(8,128)(2,1)} %copy-done.23, ...), custom_call_target="tpu_custom_call" | custom-call | flops 4831838208 | bytes 4831838 | tf_op jit(solution)/shard_map/grad_terms/pallas_call | solution.py:127
  238.2 3.6 collective-permute-done.16
  241.8 3.1 add_convert_fusion
  244.9 3.1 collective-permute-start.17
  251.4 4.6 %collective-permute-start.20 = (bf16[64,1536]{1,0:T(8,128)(2,1)S(1)}, bf16[64,1536]{1,0:T(8,128)(2,1)}, u32[]{:S(2)}, u32[]{:S(2)}) collective-permute-start(bf16[64,1536]{1,0:T(8,128)(2,1)S(1)} %copy-done.32), channel_id=1, source_target_pairs={{2,0},{7,1},{8,2},{13,3},{3,4},{6,5},{9,6},{12,7},{0,8},{5,9},{10,... | collective-permute-start | bytes 589832 | tf_op jit(solution)/shard_map/ppermute | solution.py:56
  255.9 4.2 collective-permute-start.21
  260.1 9.5 %grad_terms.8 = (bf16[2,64,3072]{2,1,0:T(8,128)(2,1)}, f32[2,64,3072]{2,1,0:T(8,128)}, bf16[256,1536]{1,0:T(8,128)(2,1)}) custom-call(s32[4]{0:T(128)} %iota_xor_fusion.2.place.scalars, bf16[64,1536]{1,0:T(8,128)(2,1)} %copy-done.28, bf16[64,1536]{1,0:T(8,128)(2,1)} %copy-done.29, bf16[64,1536]{1,0:T(8,128)(2,1)} %copy-done.30, bf16[64,1536]{1,0:T(8,128)(2,1)} %copy-done.31, ...), custom_call_target="tpu_custom_call" | custom-call | flops 2415919104 | bytes 2415919 | tf_op jit(solution)/shard_map/grad_terms/pallas_call | solution.py:127
  269.6 5.0 %collective-permute-done.20.refs_2_ = bf16[64,1536]{1,0:T(8,128)(2,1)} collective-permute-done((bf16[64,1536]{1,0:T(8,128)(2,1)S(1)}, bf16[64,1536]{1,0:T(8,128)(2,1)}, u32[]{:S(2)}, u32[]{:S(2)}) %collective-permute-start.20) | collective-permute-done | bytes 196640 | tf_op jit(solution)/shard_map/ppermute | solution.py:56
  274.6 3.1 fusion
  280.9 3.0 collective-permute-start.24
  284.6 9.5 %grad_terms.9 = (bf16[2,64,3072]{2,1,0:T(8,128)(2,1)}, f32[2,64,3072]{2,1,0:T(8,128)}, bf16[256,1536]{1,0:T(8,128)(2,1)}) custom-call(s32[4]{0:T(128)} %iota_xor_fusion.2.place.scalars, bf16[64,1536]{1,0:T(8,128)(2,1)} %collective-permute-done.18.refs_0_, bf16[64,1536]{1,0:T(8,128)(2,1)} %collective-permute-done.19.refs_1_, ...), custom_call_target="tpu_custom_call" | custom-call | flops 2415919104 | bytes 2415919 | tf_op jit(solution)/shard_map/grad_terms/pallas_call | solution.py:127
  294.0 5.9 %collective-permute-done.22.refs_0_ = bf16[128,3072]{1,0:T(8,128)(2,1)} collective-permute-done((bf16[128,3072]{1,0:T(8,128)(2,1)}, bf16[128,3072]{1,0:T(8,128)(2,1)}, u32[]{:S(2)}, u32[]{:S(2)}) %collective-permute-start.22) | collective-permute-done | bytes 786464 | tf_op jit(solution)/shard_map/ppermute | solution.py:50
  299.9 4.9 %collective-permute-start.25 = (bf16[128,3072]{1,0:T(8,128)(2,1)}, bf16[128,3072]{1,0:T(8,128)(2,1)}, u32[]{:S(2)}, u32[]{:S(2)}) collective-permute-start(bf16[128,3072]{1,0:T(8,128)(2,1)} %collective-permute-done.22.refs_0_), channel_id=1, source_target_pairs={{0,2},{1,3},{2,0},{3,1},{4,6},{5,7},{6,4},{7,5},{8,10},{9,11},{10,... | collective-permute-start | bytes 2359304 | tf_op jit(solution)/shard_map/ppermute | solution.py:44
  311.3 2.5 broadcast_select_fusion
  314.8 15.7 %outer.7.into_ref = bf16[3072,4608]{1,0:T(8,128)(2,1)} custom-call(s32[4]{0:T(128)} %iota_xor_fusion.2.place.scalars, bf16[3072,4608]{1,0:T(8,128)(2,1)} %outer.6.into_ref, bf16[3072,1024]{1,0:T(8,128)(2,1)} %turn.2.left_ref, bf16[1024,1536]{1,0:T(8,128)(2,1)} %get-tuple-element.110.refs_0_), custom_call_target="tpu_custom_call", output_to_operand_aliasing={{}: (1, {})} | custom-call | flops 9663676416 | bytes 9663676 | tf_op jit(solution)/shard_map/outer/pallas_call | solution.py:220
  330.9 3.9 collective-permute-start.31
  336.8 2.4 collective-permute-start.30
  339.2 2.3 fusion.2
  342.8 2.5 fusion.1
  345.3 12.2 %attn_terms.3 = (bf16[2,128,1536]{2,1,0:T(8,128)(2,1)}, f32[2,128,1536]{2,1,0:T(8,128)}, bf16[4,128,3072]{2,1,0:T(8,128)(2,1)}) custom-call(s32[9]{0:T(128)} %pad_add_fusion.scalars, bf16[128,3072]{1,0:T(8,128)(2,1)} %collective-permute-done.22.refs_0_, bf16[128,3072]{1,0:T(8,128)(2,1)} %collective-permute-done.29.refs_1_, ...), custom_call_target="tpu_custom_call" | custom-call | flops 4831838208 | bytes 4831838 | tf_op jit(solution)/shard_map/attn_terms/pallas_call | solution.py:172
  367.3 8.8 %attn_terms.4 = (bf16[2,64,1536]{2,1,0:T(8,128)(2,1)}, f32[2,64,1536]{2,1,0:T(8,128)}, bf16[4,64,3072]{2,1,0:T(8,128)(2,1)}) custom-call(s32[9]{0:T(128)} %pad_add_fusion.scalars, bf16[64,3072]{1,0:T(8,128)(2,1)} %copy-done.12, bf16[64,3072]{1,0:T(8,128)(2,1)} %collective-permute-done.35.refs_1_, bf16[64,3072]{1,0:T(8,128)(2,1)} %collective-permute-done.31.refs_2_, ...), custom_call_target="tpu_custom_call" | custom-call | flops 2415919104 | bytes 2415919 | tf_op jit(solution)/shard_map/attn_terms/pallas_call | solution.py:172
  376.2 10.6 %outer.8.into_ref = bf16[3072,4608]{1,0:T(8,128)(2,1)} custom-call(s32[4]{0:T(128)} %iota_xor_fusion.2.place.scalars, bf16[3072,4608]{1,0:T(8,128)(2,1)} %outer.7.into_ref, bf16[3072,1024]{1,0:T(8,128)(2,1)} %turn.2.left_ref, bf16[512,1536]{1,0:T(8,128)(2,1)} %get-tuple-element.124.refs_0_, ...), custom_call_target="tpu_custom_call", output_to_operand_aliasing={{}: (1, {})} | custom-call | flops 4831838208 | bytes 4831838 | tf_op jit(solution)/shard_map/outer/pallas_call | solution.py:220
  386.7 2.7 collective-permute-start.40
  395.7 9.0 %attn_terms.5 = (bf16[2,64,1536]{2,1,0:T(8,128)(2,1)}, f32[2,64,1536]{2,1,0:T(8,128)}, bf16[4,64,3072]{2,1,0:T(8,128)(2,1)}) custom-call(s32[9]{0:T(128)} %pad_add_fusion.scalars, bf16[64,3072]{1,0:T(8,128)(2,1)} %copy-done.11, bf16[64,3072]{1,0:T(8,128)(2,1)} %collective-permute-done.39.refs_1_, bf16[64,3072]{1,0:T(8,128)(2,1)} %collective-permute-done.34.refs_2_, ...), custom_call_target="tpu_custom_call" | custom-call | flops 2415919104 | bytes 2415919 | tf_op jit(solution)/shard_map/attn_terms/pallas_call | solution.py:172
  405.4 7.8 %collective-permute-done.37 = bf16[1,128,1536]{2,1,0:T(8,128)(2,1)} collective-permute-done((bf16[1,128,1536]{2,1,0:T(8,128)(2,1)}, bf16[1,128,1536]{2,1,0:T(8,128)(2,1)}, u32[]{:S(2)}, u32[]{:S(2)}) %collective-permute-start.37) | collective-permute-done | bytes 393248 | tf_op jit(solution)/shard_map/ppermute | solution.py:34
  415.5 10.5 %outer.9 = bf16[3072,4608]{1,0:T(8,128)(2,1)} custom-call(s32[4]{0:T(128)} %iota_xor_fusion.2.place.scalars, bf16[3072,4608]{1,0:T(8,128)(2,1)} %outer.8.into_ref, bf16[3072,1024]{1,0:T(8,128)(2,1)} %turn.2.left_ref, bf16[512,1536]{1,0:T(8,128)(2,1)} %get-tuple-element.124.refs_0_, ...), custom_call_target="tpu_custom_call", output_to_operand_aliasing={{}: (1, {})} | custom-call | flops 4831838208 | bytes 4831838 | tf_op jit(solution)/shard_map/outer/pallas_call | solution.py:220
  427.3 10.5 %outer.10.into_ref = bf16[1536,3072]{1,0:T(8,128)(2,1)} custom-call(s32[4]{0:T(128)} %iota_xor_fusion.2.place.scalars, bf16[1536,1024]{1,0:T(8,128)(2,1)} %turn.3.left_ref, bf16[512,3072]{1,0:T(8,128)(2,1)} %bitcast.65, bf16[256,3072]{1,0:T(8,128)(2,1)} %bitcast.68, bf16[256,3072]{1,0:T(8,128)(2,1)} %bitcast.70), custom_call_target="tpu_custom_call" | custom-call | flops 4831838208 | bytes 4831838 | tf_op jit(solution)/shard_map/outer/pallas_call | solution.py:220
  437.8 2.4 collective-permute-done.42
  440.4 10.4 %outer.11 = bf16[1536,3072]{1,0:T(8,128)(2,1)} custom-call(s32[4]{0:T(128)} %iota_xor_fusion.2.place.scalars, bf16[1536,3072]{1,0:T(8,128)(2,1)} %outer.10.into_ref, bf16[1536,1024]{1,0:T(8,128)(2,1)} %turn.3.left_ref, bf16[512,3072]{1,0:T(8,128)(2,1)} %bitcast.66, bf16[256,3072]{1,0:T(8,128)(2,1)} %bitcast.69, ...), custom_call_target="tpu_custom_call", output_to_operand_aliasing={{}: (1, {})} | custom-call | flops 4831838208 | bytes 4831838 | tf_op jit(solution)/shard_map/outer/pallas_call | solution.py:220
  (154 shorter events, 53.3 us)
Async XLA Ops:
  2.1 34.1 %collective-permute-start = (bf16[256,1536]{1,0:T(8,128)(2,1)S(1)}, bf16[256,1536]{1,0:T(8,128)(2,1)S(1)}, u32[]{:S(2)}, u32[]{:S(2)}) collective-permute-start(bf16[256,1536]{1,0:T(8,128)(2,1)S(1)} %get-tuple-element.156), channel_id=1, source_target_pairs={{0,0},{5,1},{10,2},{15,3},{1,4},{4,5},{11,6},{14,7},{2,8},{7,9},{8... | collective-permute-start | bytes 2359304 | tf_op jit(solution)/shard_map/ppermute | solution.py:56
  2.8 33.3 %collective-permute-start.1 = (bf16[256,1536]{1,0:T(8,128)(2,1)S(1)}, bf16[256,1536]{1,0:T(8,128)(2,1)S(1)}, u32[]{:S(2)}, u32[]{:S(2)}) collective-permute-start(bf16[256,1536]{1,0:T(8,128)(2,1)S(1)} %get-tuple-element.156), channel_id=1, source_target_pairs={{1,0},{4,1},{11,2},{14,3},{0,4},{5,5},{10,6},{15,7},{3,8},{6,9},{9... | collective-permute-start | bytes 2359304 | tf_op jit(solution)/shard_map/ppermute | solution.py:56
  9.0 39.8 %collective-permute-start.2 = (bf16[256,1536]{1,0:T(8,128)(2,1)S(1)}, bf16[256,1536]{1,0:T(8,128)(2,1)}, u32[]{:S(2)}, u32[]{:S(2)}) collective-permute-start(bf16[256,1536]{1,0:T(8,128)(2,1)S(1)} %get-tuple-element.156), channel_id=1, source_target_pairs={{2,0},{7,1},{8,2},{13,3},{3,4},{6,5},{9,6},{12,7},{0,8},{5,9},{10,... | collective-permute-start | bytes 2359304 | tf_op jit(solution)/shard_map/ppermute | solution.py:56
  14.4 43.7 %collective-permute-start.3 = (bf16[256,1536]{1,0:T(8,128)(2,1)S(1)}, bf16[256,1536]{1,0:T(8,128)(2,1)}, u32[]{:S(2)}, u32[]{:S(2)}) collective-permute-start(bf16[256,1536]{1,0:T(8,128)(2,1)S(1)} %get-tuple-element.156), channel_id=1, source_target_pairs={{3,0},{6,1},{9,2},{12,3},{2,4},{7,5},{8,6},{13,7},{1,8},{4,9},{11,... | collective-permute-start | bytes 2359304 | tf_op jit(solution)/shard_map/ppermute | solution.py:56
  58.1 72.3 %collective-permute-start.4 = (bf16[256,1536]{1,0:T(8,128)(2,1)S(1)}, bf16[256,1536]{1,0:T(8,128)(2,1)S(1)}, u32[]{:S(2)}, u32[]{:S(2)}) collective-permute-start(bf16[256,1536]{1,0:T(8,128)(2,1)S(1)} %get-tuple-element.79), channel_id=1, source_target_pairs={{0,0},{5,1},{10,2},{15,3},{1,4},{4,5},{11,6},{14,7},{2,8},{7,9},{8... | collective-permute-start | bytes 2359304 | tf_op jit(solution)/shard_map/ppermute | solution.py:56
  58.9 71.6 %collective-permute-start.5 = (bf16[256,1536]{1,0:T(8,128)(2,1)S(1)}, bf16[256,1536]{1,0:T(8,128)(2,1)S(1)}, u32[]{:S(2)}, u32[]{:S(2)}) collective-permute-start(bf16[256,1536]{1,0:T(8,128)(2,1)S(1)} %get-tuple-element.79), channel_id=1, source_target_pairs={{1,0},{4,1},{11,2},{14,3},{0,4},{5,5},{10,6},{15,7},{3,8},{6,9},{9... | collective-permute-start | bytes 2359304 | tf_op jit(solution)/shard_map/ppermute | solution.py:56
  86.6 43.9 %collective-permute-start.6 = (bf16[256,1536]{1,0:T(8,128)(2,1)S(1)}, bf16[256,1536]{1,0:T(8,128)(2,1)S(1)}, u32[]{:S(2)}, u32[]{:S(2)}) collective-permute-start(bf16[256,1536]{1,0:T(8,128)(2,1)S(1)} %get-tuple-element.79), channel_id=1, source_target_pairs={{2,0},{7,1},{8,2},{13,3},{3,4},{6,5},{9,6},{12,7},{0,8},{5,9},{10,... | collective-permute-start | bytes 2359304 | tf_op jit(solution)/shard_map/ppermute | solution.py:56
  92.1 43.5 %collective-permute-start.7 = (bf16[256,1536]{1,0:T(8,128)(2,1)S(1)}, bf16[256,1536]{1,0:T(8,128)(2,1)}, u32[]{:S(2)}, u32[]{:S(2)}) collective-permute-start(bf16[256,1536]{1,0:T(8,128)(2,1)S(1)} %get-tuple-element.79), channel_id=1, source_target_pairs={{3,0},{6,1},{9,2},{12,3},{2,4},{7,5},{8,6},{13,7},{1,8},{4,9},{11,... | collective-permute-start | bytes 2359304 | tf_op jit(solution)/shard_map/ppermute | solution.py:56
  130.4 48.2 %copy-start.20 = (bf16[256,1536]{1,0:T(8,128)(2,1)}, bf16[256,1536]{1,0:T(8,128)(2,1)S(1)}, u32[]{:S(2)}) copy-start(bf16[256,1536]{1,0:T(8,128)(2,1)S(1)} %collective-permute-done.4.refs_0_) | copy-start | bytes 2359300
  130.5 48.2 %copy-start.21 = (bf16[256,1536]{1,0:T(8,128)(2,1)}, bf16[256,1536]{1,0:T(8,128)(2,1)S(1)}, u32[]{:S(2)}) copy-start(bf16[256,1536]{1,0:T(8,128)(2,1)S(1)} %collective-permute-done.5.refs_1_) | copy-start | bytes 2359300
  130.5 48.2 %copy-start.22 = (bf16[256,1536]{1,0:T(8,128)(2,1)}, bf16[256,1536]{1,0:T(8,128)(2,1)S(1)}, u32[]{:S(2)}) copy-start(bf16[256,1536]{1,0:T(8,128)(2,1)S(1)} %collective-permute-done.6.refs_2_) | copy-start | bytes 2359300
  135.6 62.2 %collective-permute-start.10 = (bf16[128,1536]{1,0:T(8,128)(2,1)}, bf16[128,1536]{1,0:T(8,128)(2,1)S(1)}, u32[]{:S(2)}, u32[]{:S(2)}) collective-permute-start(bf16[128,1536]{1,0:T(8,128)(2,1)} %slice.116), channel_id=1, source_target_pairs={{2,0},{7,1},{8,2},{13,3},{3,4},{6,5},{9,6},{12,7},{0,8},{5,9},{10,... | collective-permute-start | bytes 1179656 | tf_op jit(solution)/shard_map/ppermute | solution.py:56
  169.1 28.7 %collective-permute-start.11 = (bf16[128,1536]{1,0:T(8,128)(2,1)}, bf16[128,1536]{1,0:T(8,128)(2,1)S(1)}, u32[]{:S(2)}, u32[]{:S(2)}) collective-permute-start(bf16[128,1536]{1,0:T(8,128)(2,1)} %slice.116), channel_id=1, source_target_pairs={{3,0},{6,1},{9,2},{12,3},{2,4},{7,5},{8,6},{13,7},{1,8},{4,9},{11,... | collective-permute-start | bytes 1179656 | tf_op jit(solution)/shard_map/ppermute | solution.py:56
  171.1 26.8 %collective-permute-start.8 = (bf16[128,1536]{1,0:T(8,128)(2,1)}, bf16[128,1536]{1,0:T(8,128)(2,1)S(1)}, u32[]{:S(2)}, u32[]{:S(2)}) collective-permute-start(bf16[128,1536]{1,0:T(8,128)(2,1)} %slice.116), channel_id=1, source_target_pairs={{0,0},{5,1},{10,2},{15,3},{1,4},{4,5},{11,6},{14,7},{2,8},{7,9},{8... | collective-permute-start | bytes 1179656 | tf_op jit(solution)/shard_map/ppermute | solution.py:56
  172.7 25.2 %collective-permute-start.9 = (bf16[128,1536]{1,0:T(8,128)(2,1)}, bf16[128,1536]{1,0:T(8,128)(2,1)S(1)}, u32[]{:S(2)}, u32[]{:S(2)}) collective-permute-start(bf16[128,1536]{1,0:T(8,128)(2,1)} %slice.116), channel_id=1, source_target_pairs={{1,0},{4,1},{11,2},{14,3},{0,4},{5,5},{10,6},{15,7},{3,8},{6,9},{9... | collective-permute-start | bytes 1179656 | tf_op jit(solution)/shard_map/ppermute | solution.py:56
  197.9 40.2 %collective-permute-start.12 = (bf16[64,1536]{1,0:T(8,128)(2,1)}, bf16[64,1536]{1,0:T(8,128)(2,1)S(1)}, u32[]{:S(2)}, u32[]{:S(2)}) collective-permute-start(bf16[64,1536]{1,0:T(8,128)(2,1)} %get-tuple-element.90), channel_id=1, source_target_pairs={{0,0},{5,1},{10,2},{15,3},{1,4},{4,5},{11,6},{14,7},{2,8},{7,9},{8... | collective-permute-start | bytes 589832 | tf_op jit(solution)/shard_map/ppermute | solution.py:56
  199.5 38.6 %collective-permute-start.13 = (bf16[64,1536]{1,0:T(8,128)(2,1)}, bf16[64,1536]{1,0:T(8,128)(2,1)S(1)}, u32[]{:S(2)}, u32[]{:S(2)}) collective-permute-start(bf16[64,1536]{1,0:T(8,128)(2,1)} %get-tuple-element.90), channel_id=1, source_target_pairs={{1,0},{4,1},{11,2},{14,3},{0,4},{5,5},{10,6},{15,7},{3,8},{6,9},{9... | collective-permute-start | bytes 589832 | tf_op jit(solution)/shard_map/ppermute | solution.py:56
  204.2 33.9 %collective-permute-start.14 = (bf16[64,1536]{1,0:T(8,128)(2,1)}, bf16[64,1536]{1,0:T(8,128)(2,1)S(1)}, u32[]{:S(2)}, u32[]{:S(2)}) collective-permute-start(bf16[64,1536]{1,0:T(8,128)(2,1)} %get-tuple-element.90), channel_id=1, source_target_pairs={{2,0},{7,1},{8,2},{13,3},{3,4},{6,5},{9,6},{12,7},{0,8},{5,9},{10,... | collective-permute-start | bytes 589832 | tf_op jit(solution)/shard_map/ppermute | solution.py:56
  220.6 17.5 %collective-permute-start.15 = (bf16[64,1536]{1,0:T(8,128)(2,1)}, bf16[64,1536]{1,0:T(8,128)(2,1)S(1)}, u32[]{:S(2)}, u32[]{:S(2)}) collective-permute-start(bf16[64,1536]{1,0:T(8,128)(2,1)} %get-tuple-element.90), channel_id=1, source_target_pairs={{3,0},{6,1},{9,2},{12,3},{2,4},{7,5},{8,6},{13,7},{1,8},{4,9},{11,... | collective-permute-start | bytes 589832 | tf_op jit(solution)/shard_map/ppermute | solution.py:56
  238.1 3.7 collective-permute-start.16
  244.9 29.6 %collective-permute-start.17 = (bf16[1,128,3072]{2,1,0:T(8,128)(2,1)}, bf16[1,128,3072]{2,1,0:T(8,128)(2,1)}, u32[]{:S(2)}, u32[]{:S(2)}) collective-permute-start(bf16[1,128,3072]{2,1,0:T(8,128)(2,1)} %add_convert_fusion), channel_id=1, source_target_pairs={{0,2},{1,3},{2,0},{3,1},{4,6},{5,7},{6,4},{7,5},{8,10},{9,11},{10,... | collective-permute-start | bytes 2359304 | tf_op jit(solution)/shard_map/ppermute | solution.py:34
  248.0 21.6 %collective-permute-start.18 = (bf16[64,1536]{1,0:T(8,128)(2,1)S(1)}, bf16[64,1536]{1,0:T(8,128)(2,1)}, u32[]{:S(2)}, u32[]{:S(2)}) collective-permute-start(bf16[64,1536]{1,0:T(8,128)(2,1)S(1)} %copy-done.32), channel_id=1, source_target_pairs={{0,0},{5,1},{10,2},{15,3},{1,4},{4,5},{11,6},{14,7},{2,8},{7,9},{8... | collective-permute-start | bytes 589832 | tf_op jit(solution)/shard_map/ppermute | solution.py:56
  249.4 20.2 %collective-permute-start.19 = (bf16[64,1536]{1,0:T(8,128)(2,1)S(1)}, bf16[64,1536]{1,0:T(8,128)(2,1)}, u32[]{:S(2)}, u32[]{:S(2)}) collective-permute-start(bf16[64,1536]{1,0:T(8,128)(2,1)S(1)} %copy-done.32), channel_id=1, source_target_pairs={{1,0},{4,1},{11,2},{14,3},{0,4},{5,5},{10,6},{15,7},{3,8},{6,9},{9... | collective-permute-start | bytes 589832 | tf_op jit(solution)/shard_map/ppermute | solution.py:56
  251.4 23.2 %collective-permute-start.20 = (bf16[64,1536]{1,0:T(8,128)(2,1)S(1)}, bf16[64,1536]{1,0:T(8,128)(2,1)}, u32[]{:S(2)}, u32[]{:S(2)}) collective-permute-start(bf16[64,1536]{1,0:T(8,128)(2,1)S(1)} %copy-done.32), channel_id=1, source_target_pairs={{2,0},{7,1},{8,2},{13,3},{3,4},{6,5},{9,6},{12,7},{0,8},{5,9},{10,... | collective-permute-start | bytes 589832 | tf_op jit(solution)/shard_map/ppermute | solution.py:56
  255.9 18.6 %collective-permute-start.21 = (bf16[64,1536]{1,0:T(8,128)(2,1)S(1)}, bf16[64,1536]{1,0:T(8,128)(2,1)}, u32[]{:S(2)}, u32[]{:S(2)}) collective-permute-start(bf16[64,1536]{1,0:T(8,128)(2,1)S(1)} %copy-done.32), channel_id=1, source_target_pairs={{3,0},{6,1},{9,2},{12,3},{2,4},{7,5},{8,6},{13,7},{1,8},{4,9},{11,... | collective-permute-start | bytes 589832 | tf_op jit(solution)/shard_map/ppermute | solution.py:56
  274.6 4.5 collective-permute-start.23
  277.7 22.3 %collective-permute-start.22 = (bf16[128,3072]{1,0:T(8,128)(2,1)}, bf16[128,3072]{1,0:T(8,128)(2,1)}, u32[]{:S(2)}, u32[]{:S(2)}) collective-permute-start(bf16[128,3072]{1,0:T(8,128)(2,1)} %fusion), channel_id=1, source_target_pairs={{16,0},{17,1},{18,2},{19,3},{20,4},{21,5},{22,6},{23,7},{24,8},{25... | collective-permute-start | bytes 2359304 | tf_op jit(solution)/shard_map/ppermute | solution.py:50
  280.9 19.0 %collective-permute-start.24 = (bf16[1,64,3072]{2,1,0:T(8,128)(2,1)}, bf16[1,64,3072]{2,1,0:T(8,128)(2,1)S(1)}, u32[]{:S(2)}, u32[]{:S(2)}) collective-permute-start(bf16[1,64,3072]{2,1,0:T(8,128)(2,1)} %add_convert_fusion.4), channel_id=1, source_target_pairs={{0,2},{1,3},{2,0},{3,1},{4,6},{5,7},{6,4},{7,5},{8,10},{9,11},{10,... | collective-permute-start | bytes 1179656 | tf_op jit(solution)/shard_map/ppermute | solution.py:34
  299.9 30.6 %collective-permute-start.25 = (bf16[128,3072]{1,0:T(8,128)(2,1)}, bf16[128,3072]{1,0:T(8,128)(2,1)}, u32[]{:S(2)}, u32[]{:S(2)}) collective-permute-start(bf16[128,3072]{1,0:T(8,128)(2,1)} %collective-permute-done.22.refs_0_), channel_id=1, source_target_pairs={{0,2},{1,3},{2,0},{3,1},{4,6},{5,7},{6,4},{7,5},{8,10},{9,11},{10,... | collective-permute-start | bytes 2359304 | tf_op jit(solution)/shard_map/ppermute | solution.py:44
  304.9 40.4 %collective-permute-start.29 = (bf16[128,3072]{1,0:T(8,128)(2,1)}, bf16[128,3072]{1,0:T(8,128)(2,1)}, u32[]{:S(2)}, u32[]{:S(2)}) collective-permute-start(bf16[128,3072]{1,0:T(8,128)(2,1)} %collective-permute-done.22.refs_0_), channel_id=1, source_target_pairs={{0,1},{1,0},{2,3},{3,2},{4,5},{5,4},{6,7},{7,6},{8,9},{9,8},{10,11... | collective-permute-start | bytes 2359304 | tf_op jit(solution)/shard_map/ppermute | solution.py:44
  306.8 6.9 %collective-permute-start.27 = (bf16[2,64,3072]{2,1,0:T(8,128)(2,1)}, bf16[2,64,3072]{2,1,0:T(8,128)(2,1)S(1)}, u32[]{:S(2)}, u32[]{:S(2)}) collective-permute-start(bf16[2,64,3072]{2,1,0:T(8,128)(2,1)} %get-tuple-element.107), channel_id=1, source_target_pairs={{0,1},{1,0},{2,3},{3,2},{4,5},{5,4},{6,7},{7,6},{8,9},{9,8},{10,11... | collective-permute-start | bytes 2359304 | tf_op jit(solution)/shard_map/ppermute | solution.py:34
  309.7 20.9 %collective-permute-start.26 = (bf16[64,3072]{1,0:T(8,128)(2,1)}, bf16[64,3072]{1,0:T(8,128)(2,1)S(1)}, u32[]{:S(2)}, u32[]{:S(2)}) collective-permute-start(bf16[64,3072]{1,0:T(8,128)(2,1)} %fusion.4), channel_id=1, source_target_pairs={{16,0},{17,1},{18,2},{19,3},{20,4},{21,5},{22,6},{23,7},{24,8},{25... | collective-permute-start | bytes 1179656 | tf_op jit(solution)/shard_map/ppermute | solution.py:50
  314.8 16.1 %collective-permute-start.28 = (bf16[1,64,3072]{2,1,0:T(8,128)(2,1)}, bf16[1,64,3072]{2,1,0:T(8,128)(2,1)S(1)}, u32[]{:S(2)}, u32[]{:S(2)}) collective-permute-start(bf16[1,64,3072]{2,1,0:T(8,128)(2,1)} %add_convert_fusion.3), channel_id=1, source_target_pairs={{0,2},{1,3},{2,0},{3,1},{4,6},{5,7},{6,4},{7,5},{8,10},{9,11},{10,... | collective-permute-start | bytes 1179656 | tf_op jit(solution)/shard_map/ppermute | solution.py:34
  330.5 29.8 %copy-start.12 = (bf16[64,3072]{1,0:T(8,128)(2,1)}, bf16[64,3072]{1,0:T(8,128)(2,1)S(1)}, u32[]{:S(2)}) copy-start(bf16[64,3072]{1,0:T(8,128)(2,1)S(1)} %collective-permute-done.26.refs_0_) | copy-start | bytes 1179652
  330.9 26.6 %collective-permute-start.31 = (bf16[64,3072]{1,0:T(8,128)(2,1)S(1)}, bf16[64,3072]{1,0:T(8,128)(2,1)}, u32[]{:S(2)}, u32[]{:S(2)}) collective-permute-start(bf16[64,3072]{1,0:T(8,128)(2,1)S(1)} %collective-permute-done.26.refs_0_), channel_id=1, source_target_pairs={{0,2},{1,3},{2,0},{3,1},{4,6},{5,7},{6,4},{7,5},{8,10},{9,11},{10,... | collective-permute-start | bytes 1179656 | tf_op jit(solution)/shard_map/ppermute | solution.py:44
  334.8 31.7 %collective-permute-start.35 = (bf16[64,3072]{1,0:T(8,128)(2,1)S(1)}, bf16[64,3072]{1,0:T(8,128)(2,1)}, u32[]{:S(2)}, u32[]{:S(2)}) collective-permute-start(bf16[64,3072]{1,0:T(8,128)(2,1)S(1)} %collective-permute-done.26.refs_0_), channel_id=1, source_target_pairs={{0,1},{1,0},{2,3},{3,2},{4,5},{5,4},{6,7},{7,6},{8,9},{9,8},{10,11... | collective-permute-start | bytes 1179656 | tf_op jit(solution)/shard_map/ppermute | solution.py:44
  336.8 8.5 %collective-permute-start.30 = (bf16[128,3072]{1,0:T(8,128)(2,1)}, bf16[128,3072]{1,0:T(8,128)(2,1)}, u32[]{:S(2)}, u32[]{:S(2)}) collective-permute-start(bf16[128,3072]{1,0:T(8,128)(2,1)} %collective-permute-done.25.refs_2_), channel_id=1, source_target_pairs={{0,1},{1,0},{2,3},{3,2},{4,5},{5,4},{6,7},{7,6},{8,9},{9,8},{10,11... | collective-permute-start | bytes 2359304 | tf_op jit(solution)/shard_map/ppermute | solution.py:44
  341.5 16.0 %collective-permute-start.32 = (bf16[64,3072]{1,0:T(8,128)(2,1)}, bf16[64,3072]{1,0:T(8,128)(2,1)S(1)}, u32[]{:S(2)}, u32[]{:S(2)}) collective-permute-start(bf16[64,3072]{1,0:T(8,128)(2,1)} %fusion.2), channel_id=1, source_target_pairs={{16,0},{17,1},{18,2},{19,3},{20,4},{21,5},{22,6},{23,7},{24,8},{25... | collective-permute-start | bytes 1179656 | tf_op jit(solution)/shard_map/ppermute | solution.py:50
  357.5 9.0 %collective-permute-start.36 = (bf16[64,3072]{1,0:T(8,128)(2,1)}, bf16[64,3072]{1,0:T(8,128)(2,1)S(1)}, u32[]{:S(2)}, u32[]{:S(2)}) collective-permute-start(bf16[64,3072]{1,0:T(8,128)(2,1)} %collective-permute-done.31.refs_2_), channel_id=1, source_target_pairs={{0,1},{1,0},{2,3},{3,2},{4,5},{5,4},{6,7},{7,6},{8,9},{9,8},{10,11... | collective-permute-start | bytes 1179656 | tf_op jit(solution)/shard_map/ppermute | solution.py:44
  359.4 27.3 %collective-permute-start.33 = (bf16[2,128,1536]{2,1,0:T(8,128)(2,1)}, bf16[2,128,1536]{2,1,0:T(8,128)(2,1)}, u32[]{:S(2)}, u32[]{:S(2)}) collective-permute-start(bf16[2,128,1536]{2,1,0:T(8,128)(2,1)} %get-tuple-element.118), channel_id=1, source_target_pairs={{0,4},{4,0},{8,12},{12,8},{1,5},{5,1},{9,13},{13,9},{2,6},{6,2},{1... | collective-permute-start | bytes 2359304 | tf_op jit(solution)/shard_map/ppermute | solution.py:34
  362.4 24.3 %collective-permute-start.34 = (bf16[64,3072]{1,0:T(8,128)(2,1)S(1)}, bf16[64,3072]{1,0:T(8,128)(2,1)}, u32[]{:S(2)}, u32[]{:S(2)}) collective-permute-start(bf16[64,3072]{1,0:T(8,128)(2,1)S(1)} %collective-permute-done.32.refs_0_), channel_id=1, source_target_pairs={{0,2},{1,3},{2,0},{3,1},{4,6},{5,7},{6,4},{7,5},{8,10},{9,11},{10,... | collective-permute-start | bytes 1179656 | tf_op jit(solution)/shard_map/ppermute | solution.py:44
  364.5 31.2 %collective-permute-start.39 = (bf16[64,3072]{1,0:T(8,128)(2,1)S(1)}, bf16[64,3072]{1,0:T(8,128)(2,1)}, u32[]{:S(2)}, u32[]{:S(2)}) collective-permute-start(bf16[64,3072]{1,0:T(8,128)(2,1)S(1)} %collective-permute-done.32.refs_0_), channel_id=1, source_target_pairs={{0,1},{1,0},{2,3},{3,2},{4,5},{5,4},{6,7},{7,6},{8,9},{9,8},{10,11... | collective-permute-start | bytes 1179656 | tf_op jit(solution)/shard_map/ppermute | solution.py:44
  386.7 9.0 %collective-permute-start.40 = (bf16[64,3072]{1,0:T(8,128)(2,1)}, bf16[64,3072]{1,0:T(8,128)(2,1)}, u32[]{:S(2)}, u32[]{:S(2)}) collective-permute-start(bf16[64,3072]{1,0:T(8,128)(2,1)} %collective-permute-done.34.refs_2_), channel_id=1, source_target_pairs={{0,1},{1,0},{2,3},{3,2},{4,5},{5,4},{6,7},{7,6},{8,9},{9,8},{10,11... | collective-permute-start | bytes 1179656 | tf_op jit(solution)/shard_map/ppermute | solution.py:44
  389.5 15.9 %collective-permute-start.38 = (bf16[2,64,1536]{2,1,0:T(8,128)(2,1)}, bf16[2,64,1536]{2,1,0:T(8,128)(2,1)}, u32[]{:S(2)}, u32[]{:S(2)}) collective-permute-start(bf16[2,64,1536]{2,1,0:T(8,128)(2,1)} %get-tuple-element.129), channel_id=1, source_target_pairs={{0,4},{4,0},{8,12},{12,8},{1,5},{5,1},{9,13},{13,9},{2,6},{6,2},{1... | collective-permute-start | bytes 1179656 | tf_op jit(solution)/shard_map/ppermute | solution.py:34
  392.7 20.5 %collective-permute-start.37 = (bf16[1,128,1536]{2,1,0:T(8,128)(2,1)}, bf16[1,128,1536]{2,1,0:T(8,128)(2,1)}, u32[]{:S(2)}, u32[]{:S(2)}) collective-permute-start(bf16[1,128,1536]{2,1,0:T(8,128)(2,1)} %add_convert_fusion.2), channel_id=1, source_target_pairs={{0,8},{4,12},{8,0},{12,4},{1,9},{5,13},{9,1},{13,5},{2,10},{6,14},... | collective-permute-start | bytes 1179656 | tf_op jit(solution)/shard_map/ppermute | solution.py:34
  426.0 11.8 %collective-permute-start.41 = (bf16[1,64,1536]{2,1,0:T(8,128)(2,1)S(1)}, bf16[1,64,1536]{2,1,0:T(8,128)(2,1)S(1)}, u32[]{:S(2)}, u32[]{:S(2)}) collective-permute-start(bf16[1,64,1536]{2,1,0:T(8,128)(2,1)S(1)} %add_convert_fusion.8), channel_id=1, source_target_pairs={{0,8},{4,12},{8,0},{12,4},{1,9},{5,13},{9,1},{13,5},{2,10},{6,14},... | collective-permute-start | bytes 589832 | tf_op jit(solution)/shard_map/ppermute | solution.py:34
  426.0 14.3 %collective-permute-start.42 = (bf16[2,64,1536]{2,1,0:T(8,128)(2,1)S(1)}, bf16[2,64,1536]{2,1,0:T(8,128)(2,1)S(1)}, u32[]{:S(2)}, u32[]{:S(2)}) collective-permute-start(bf16[2,64,1536]{2,1,0:T(8,128)(2,1)S(1)} %copy-done.36), channel_id=1, source_target_pairs={{0,4},{4,0},{8,12},{12,8},{1,5},{5,1},{9,13},{13,9},{2,6},{6,2},{1... | collective-permute-start | bytes 1179656 | tf_op jit(solution)/shard_map/ppermute | solution.py:34
  440.3 10.5 %collective-permute-start.43 = (bf16[1,64,1536]{2,1,0:T(8,128)(2,1)S(1)}, bf16[1,64,1536]{2,1,0:T(8,128)(2,1)S(1)}, u32[]{:S(2)}, u32[]{:S(2)}) collective-permute-start(bf16[1,64,1536]{2,1,0:T(8,128)(2,1)S(1)} %add_convert_fusion.7), channel_id=1, source_target_pairs={{0,8},{4,12},{8,0},{12,4},{1,9},{5,13},{9,1},{13,5},{2,10},{6,14},... | collective-permute-start | bytes 589832 | tf_op jit(solution)/shard_map/ppermute | solution.py:34
  (33 other events, 426.2 us)

commit v2 on v1

--- a/solution.py
+++ b/solution.py
@@ -7,8 +7,8 @@
 from jax.experimental.pallas import tpu as pltpu
 from jax.sharding import PartitionSpec as P
 
-CHUNKS = (2, 1, 1)
-PIECES = 3
+CHUNKS = (1, 1)
+PIECES = (1, 1)
 VMEM = 60 * 2**20
 BF16 = jnp.bfloat16
 F32 = jnp.float32
@@ -120,6 +120,7 @@
     bn = fitting(width, 128, 512)
     more = total is not None
     chunk = first // rows
+    piece = piece[0] // piece[1]
     keep = pl.BlockSpec((n // 2, rows, bn), lambda i, place: (0, 0, i))
     whole = pl.BlockSpec((n, rows, bn), lambda i, place: (0, 0, i))
     half = (n // 2, rows, width)
@@ -207,7 +208,7 @@
 
 def outer(scalars, left, rights, order, columns, first=0, into=None, part=(0, 1)):
     width = rights[0].shape[1] // part[1]
-    bn = fitting(width, 128, 256)
+    bn = fitting(width, 128 if width % 256 else 256, 512)
     start = part[0] * width // bn
     offset = first // bn + start
     in_specs = [pl.BlockSpec(left.shape, lambda i, s: (0, 0))] + [
@@ -252,10 +253,11 @@
         self.tasks = tasks
         token = self.token
         self.token = (*token, *before)
+        count = len(behind)
         for kernel in choose():
             made = kernel()
-            behind.append(made)
             self.token = (made,)
+            behind = behind[:count] + [made]
         self.token = tuple(behind) or token
 
 
@@ -293,11 +295,12 @@
     steps = jnp.arange(n, dtype=jnp.int32)
     token = col ^ steps
     share, columns = own.shape
-    width = columns // PIECES
+    step = columns // sum(PIECES)
+    pieces = [(sum(PIECES[:p]) * step, w * step) for p, w in enumerate(PIECES)]
     unit = share // sum(CHUNKS)
     spans = [(sum(CHUNKS[:q]) * unit, c * unit) for q, c in enumerate(CHUNKS)]
     order = [(q, d * rows, rows) for d in range(n) for q, (_, rows) in enumerate(spans)]
-    last_piece = PIECES - 1
+    last_piece = len(PIECES) - 1
 
     place = row ^ steps
     scalars = jnp.concatenate([token, row ^ col ^ steps, is_top.astype(jnp.int32)[None]])
@@ -305,9 +308,9 @@
     have = {}
 
     def gather():
-        for piece in range(PIECES):
+        for piece, (start, width) in enumerate(pieces):
             for q, (first, rows) in enumerate(spans if piece == last_piece else [(0, share)]):
-                part = own[first : first + rows, piece * width : (piece + 1) * width]
+                part = own[first : first + rows, start : start + width]
                 part = slots.gate(part)
                 blocks = [direct(part, k) for k in range(n)]
                 yield [], blocks
@@ -354,7 +357,7 @@
     def early_terms(piece):
         def run():
             have["early"], have["held", piece] = grad_terms(
-                slots.gate(place), have["blocks", piece, 0], weight, piece, have.get("early")
+                slots.gate(place), have["blocks", piece, 0], weight, pieces[piece], have.get("early")
             )
             return have["early"]
 
@@ -368,7 +371,7 @@
                 [have["held", piece]],
                 [(0, 0, n * share)],
                 columns,
-                piece * width,
+                pieces[piece][0],
                 have.get("grad"),
             )
             return have["grad"]
@@ -381,7 +384,7 @@
                 slots.gate(place),
                 have["blocks", last_piece, q],
                 weight,
-                last_piece,
+                pieces[last_piece],
                 have["early"],
                 spans[q][0],
                 True,
@@ -400,7 +403,7 @@
                 [have["late", q] for q in range(len(spans))],
                 order,
                 columns,
-                last_piece * width,
+                pieces[last_piece][0],
                 have["grad"],
                 part,
             )
@@ -438,18 +441,23 @@
 
     terms = [late_terms(q) for q in range(len(spans))]
     attns = [attn(q) for q in range(len(spans))]
-    spare = [early_grad(last_piece - 1), late_grad(0, 2), late_grad(1, 2)]
-    outs = [out_grad(0, 2), out_grad(1, 2)]
+    spare = [early_grad(last_piece - 1), *[late_grad(part, 3) for part in range(3)]]
+    outs = [out_grad(0, 1)]
 
     def late():
         if terms:
-            return [terms.pop(0)]
+            return [terms.pop(0)] + [spare.pop(0) for _ in spare[:1] if len(spare) == 4]
         if attns and ("upper", len(spans) - len(attns)) in have:
             more = len(attns) < len(spans) and len(attns) > 1
             return [attns.pop(0)] + [spare.pop(0) for _ in spare[: int(more)]]
         if spare and attns:
-            return [spare.pop(0)]
-        return [kernel for few in (spare, outs) for kernel in [few.pop(0) for _ in few[:1]]]
+            return [spare.pop(0) for _ in spare[: max(1, len(spare) - 1)]]
+        if attns:
+            return []
+        final = spare + outs
+        spare.clear()
+        outs.clear()
+        return final
 
     slots.tasks.append(gather())
     slots.run(lambda: [turn("inputs", qkv_input[0]), turn("attn_out", attn_out[0])])

time: 455 us -> 419 us (0.921)
  waiting for transfers between devices: 53 us -> 96.7 us
  starting transfers between devices: 178 us -> 136 us
  Pallas kernels: 183 us -> 157 us
  other arithmetic: 31.3 us -> 24.3 us
    ppermute x20 -> x12, starting transfers between devices: 139 us -> 99.1 us  [direct(): return lax.ppermute(block, ('row', 'col'), route)]
    ppermute x20 -> x12, waiting for transfers between devices: 32.1 us -> 53.2 us  [direct(): return lax.ppermute(block, ('row', 'col'), route)]
    ppermute x12 -> x8, waiting for transfers between devices: 14.9 us -> 34.3 us  [swap(): return lax.ppermute(block, axis, route)]
    pallas_call x5 -> x3, Pallas kernels: 67.4 us -> 52.6 us  [grad_terms(): pl.pallas_call(functools.partial(terms_kernel, n, more, split), out_shape...]
    ppermute x9 -> x6, starting transfers between devices: 23.7 us -> 13.6 us  [swap_below(): return lax.ppermute(block, ('section', 'col'), route)]
    ppermute x12 -> x8, starting transfers between devices: 10.3 us -> 20.4 us  [swap(): return lax.ppermute(block, axis, route)]
    ppermute x9 -> x6, waiting for transfers between devices: 0.02 us -> 6.98 us  [swap_below(): return lax.ppermute(block, ('section', 'col'), route)]
    pallas_call x6 -> x5, Pallas kernels: 73.5 us -> 67.3 us  [outer(): pl.pallas_call(functools.partial(kernel, order), out_shape=shape((left.sh...]
  transfers between devices with their start and end apart: 44 -> 28, of which waited for: 10 -> 12; matrix products, arithmetic and copies ran while one was open for 6% -> 4% of each run, Pallas kernels for 38% -> 38%
where the time goes in v2:
time: 419 us; the launch traced here: 418 us
  Pallas kernels  157 us (37%)
  starting transfers between devices  136 us (32%)
  waiting for transfers between devices  96.7 us (23%)
  other arithmetic  24.3 us (6%)
    ppermute x12, starting transfers between devices, direct(): return lax.ppermute(block, ('row', 'col'), route)  99.1 us
    pallas_call x5, Pallas kernels, outer(): pl.pallas_call(functools.partial(kernel, order), out_shape=shape((left.sh...  67.3 us
    ppermute x12, waiting for transfers between devices, direct(): return lax.ppermute(block, ('row', 'col'), route)  53.2 us
    pallas_call x3, Pallas kernels, grad_terms(): pl.pallas_call(functools.partial(terms_kernel, n, more, split), out_shape...  52.6 us
    ppermute x8, waiting for transfers between devices, swap(): return lax.ppermute(block, axis, route)  34.3 us
    pallas_call x2, Pallas kernels, attn_terms(): pl.pallas_call(functools.partial(attn_kernel, n), out_shape=[shape(half,...  24.5 us
    ppermute x8, starting transfers between devices, swap(): return lax.ppermute(block, axis, route)  20.4 us
    ppermute x6, starting transfers between devices, swap_below(): return lax.ppermute(block, ('section', 'col'), route)  13.6 us
  transfers between devices with their start and end apart: 28, of which 12 were waited for; matrix products, arithmetic and copies ran while one was open for 4% of the time, Pallas kernels for 38%

profile of v2, /device:TPU:0, one launch (start us, length us, event | category | flops | bytes accessed | tf_op | source)
XLA Modules:
  0.0 417.6 jit_solution(1511736940816526622)
XLA Ops:
  2.0 1.7 collective-permute-start
  3.7 5.2 %collective-permute-start.1 = (bf16[256,2304]{1,0:T(8,128)(2,1)S(1)}, bf16[256,2304]{1,0:T(8,128)(2,1)}, u32[]{:S(2)}, u32[]{:S(2)}) collective-permute-start(bf16[256,2304]{1,0:T(8,128)(2,1)S(1)} %slice.77), channel_id=1, source_target_pairs={{1,0},{4,1},{11,2},{14,3},{0,4},{5,5},{10,6},{15,7},{3,8},{6,9},{9... | collective-permute-start | bytes 3538952 | tf_op jit(solution)/shard_map/ppermute | solution.py:56
  8.9 5.5 %collective-permute-start.2 = (bf16[256,2304]{1,0:T(8,128)(2,1)S(1)}, bf16[256,2304]{1,0:T(8,128)(2,1)}, u32[]{:S(2)}, u32[]{:S(2)}) collective-permute-start(bf16[256,2304]{1,0:T(8,128)(2,1)S(1)} %slice.77), channel_id=1, source_target_pairs={{2,0},{7,1},{8,2},{13,3},{3,4},{6,5},{9,6},{12,7},{0,8},{5,9},{10,... | collective-permute-start | bytes 3538952 | tf_op jit(solution)/shard_map/ppermute | solution.py:56
  14.3 4.5 %collective-permute-start.3 = (bf16[256,2304]{1,0:T(8,128)(2,1)S(1)}, bf16[256,2304]{1,0:T(8,128)(2,1)}, u32[]{:S(2)}, u32[]{:S(2)}) collective-permute-start(bf16[256,2304]{1,0:T(8,128)(2,1)S(1)} %slice.77), channel_id=1, source_target_pairs={{3,0},{6,1},{9,2},{12,3},{2,4},{7,5},{8,6},{13,7},{1,8},{4,9},{11,... | collective-permute-start | bytes 3538952 | tf_op jit(solution)/shard_map/ppermute | solution.py:56
  19.3 7.2 %turn.2.left_ref = bf16[3072,1024]{1,0:T(8,128)(2,1)} custom-call(s32[4]{0:T(128)} %iota_xor_fusion.1.token, bf16[1024,3072]{1,0:T(8,128)(2,1)} %bitcast.47), custom_call_target="tpu_custom_call" | custom-call | flops 25165824 | bytes 25165 | tf_op jit(solution)/shard_map/turn/pallas_call | solution.py:74
  26.6 5.5 %turn.3.left_ref = bf16[1536,1024]{1,0:T(8,128)(2,1)} custom-call(s32[4]{0:T(128)} %iota_xor_fusion.1.token, bf16[1024,1536]{1,0:T(8,128)(2,1)} %bitcast.48), custom_call_target="tpu_custom_call" | custom-call | flops 12582912 | bytes 12582 | tf_op jit(solution)/shard_map/turn/pallas_call | solution.py:74
  33.5 1.8 collective-permute-done.1.refs_1_
  35.3 30.2 %collective-permute-done.2.refs_2_ = bf16[256,2304]{1,0:T(8,128)(2,1)} collective-permute-done((bf16[256,2304]{1,0:T(8,128)(2,1)S(1)}, bf16[256,2304]{1,0:T(8,128)(2,1)}, u32[]{:S(2)}, u32[]{:S(2)}) %collective-permute-start.2) | collective-permute-done | bytes 1179680 | tf_op jit(solution)/shard_map/ppermute | solution.py:56
  65.5 17.8 %collective-permute-done.3.refs_3_ = bf16[256,2304]{1,0:T(8,128)(2,1)} collective-permute-done((bf16[256,2304]{1,0:T(8,128)(2,1)S(1)}, bf16[256,2304]{1,0:T(8,128)(2,1)}, u32[]{:S(2)}, u32[]{:S(2)}) %collective-permute-start.3) | collective-permute-done | bytes 1179680 | tf_op jit(solution)/shard_map/ppermute | solution.py:56
  84.0 36.1 %collective-permute-start.5 = (bf16[128,2304]{1,0:T(8,128)(2,1)S(1)}, bf16[128,2304]{1,0:T(8,128)(2,1)S(1)}, u32[]{:S(2)}, u32[]{:S(2)}) collective-permute-start(bf16[128,2304]{1,0:T(8,128)(2,1)S(1)} %get-tuple-element.53), channel_id=1, source_target_pairs={{1,0},{4,1},{11,2},{14,3},{0,4},{5,5},{10,6},{15,7},{3,8},{6,9},{9... | collective-permute-start | bytes 1769480 | tf_op jit(solution)/shard_map/ppermute | solution.py:56
  120.1 4.2 %collective-permute-start.6 = (bf16[128,2304]{1,0:T(8,128)(2,1)S(1)}, bf16[128,2304]{1,0:T(8,128)(2,1)S(1)}, u32[]{:S(2)}, u32[]{:S(2)}) collective-permute-start(bf16[128,2304]{1,0:T(8,128)(2,1)S(1)} %get-tuple-element.53), channel_id=1, source_target_pairs={{2,0},{7,1},{8,2},{13,3},{3,4},{6,5},{9,6},{12,7},{0,8},{5,9},{10,... | collective-permute-start | bytes 1769480 | tf_op jit(solution)/shard_map/ppermute | solution.py:56
  124.3 6.6 %collective-permute-start.7 = (bf16[128,2304]{1,0:T(8,128)(2,1)S(1)}, bf16[128,2304]{1,0:T(8,128)(2,1)S(1)}, u32[]{:S(2)}, u32[]{:S(2)}) collective-permute-start(bf16[128,2304]{1,0:T(8,128)(2,1)S(1)} %get-tuple-element.53), channel_id=1, source_target_pairs={{3,0},{6,1},{9,2},{12,3},{2,4},{7,5},{8,6},{13,7},{1,8},{4,9},{11,... | collective-permute-start | bytes 1769480 | tf_op jit(solution)/shard_map/ppermute | solution.py:56
  130.9 22.2 %grad_terms.3 = (f32[4,256,3072]{2,1,0:T(8,128)}, bf16[1024,2304]{1,0:T(8,128)(2,1)}) custom-call(s32[4]{0:T(128)} %iota_xor_fusion.2.place.scalars, bf16[256,2304]{1,0:T(8,128)(2,1)} %collective-permute-done.refs_0_, bf16[256,2304]{1,0:T(8,128)(2,1)} %collective-permute-done.1.refs_1_, bf16[256,2304]{1,0:T(8,128)(2,1)} %collective-permute-done.2.refs_2_, ...), custom_call_target="tpu_custom_call" | custom-call | flops 14495514624 | bytes 14495514 | tf_op jit(solution)/shard_map/grad_terms/pallas_call | solution.py:128
  153.1 3.4 collective-permute-done.7.refs_3_
  156.6 6.0 %collective-permute-start.8 = (bf16[128,2304]{1,0:T(8,128)(2,1)}, bf16[128,2304]{1,0:T(8,128)(2,1)}, u32[]{:S(2)}, u32[]{:S(2)}) collective-permute-start(bf16[128,2304]{1,0:T(8,128)(2,1)} %get-tuple-element.59), channel_id=1, source_target_pairs={{0,0},{5,1},{10,2},{15,3},{1,4},{4,5},{11,6},{14,7},{2,8},{7,9},{8... | collective-permute-start | bytes 1769480 | tf_op jit(solution)/shard_map/ppermute | solution.py:56
  162.5 17.9 %collective-permute-start.9 = (bf16[128,2304]{1,0:T(8,128)(2,1)}, bf16[128,2304]{1,0:T(8,128)(2,1)}, u32[]{:S(2)}, u32[]{:S(2)}) collective-permute-start(bf16[128,2304]{1,0:T(8,128)(2,1)} %get-tuple-element.59), channel_id=1, source_target_pairs={{1,0},{4,1},{11,2},{14,3},{0,4},{5,5},{10,6},{15,7},{3,8},{6,9},{9... | collective-permute-start | bytes 1769480 | tf_op jit(solution)/shard_map/ppermute | solution.py:56
  180.5 4.4 %collective-permute-start.10 = (bf16[128,2304]{1,0:T(8,128)(2,1)}, bf16[128,2304]{1,0:T(8,128)(2,1)}, u32[]{:S(2)}, u32[]{:S(2)}) collective-permute-start(bf16[128,2304]{1,0:T(8,128)(2,1)} %get-tuple-element.59), channel_id=1, source_target_pairs={{2,0},{7,1},{8,2},{13,3},{3,4},{6,5},{9,6},{12,7},{0,8},{5,9},{10,... | collective-permute-start | bytes 1769480 | tf_op jit(solution)/shard_map/ppermute | solution.py:56
  184.8 6.5 %collective-permute-start.11 = (bf16[128,2304]{1,0:T(8,128)(2,1)}, bf16[128,2304]{1,0:T(8,128)(2,1)}, u32[]{:S(2)}, u32[]{:S(2)}) collective-permute-start(bf16[128,2304]{1,0:T(8,128)(2,1)} %get-tuple-element.59), channel_id=1, source_target_pairs={{3,0},{6,1},{9,2},{12,3},{2,4},{7,5},{8,6},{13,7},{1,8},{4,9},{11,... | collective-permute-start | bytes 1769480 | tf_op jit(solution)/shard_map/ppermute | solution.py:56
  191.3 15.2 %grad_terms.4 = (bf16[2,128,3072]{2,1,0:T(8,128)(2,1)}, f32[2,128,3072]{2,1,0:T(8,128)}, bf16[512,2304]{1,0:T(8,128)(2,1)}) custom-call(s32[4]{0:T(128)} %iota_xor_fusion.2.place.scalars, bf16[128,2304]{1,0:T(8,128)(2,1)} %copy-done.6, bf16[128,2304]{1,0:T(8,128)(2,1)} %copy-done.7, bf16[128,2304]{1,0:T(8,128)(2,1)} %copy-done.8, ...), custom_call_target="tpu_custom_call" | custom-call | flops 7247757312 | bytes 7247757 | tf_op jit(solution)/shard_map/grad_terms/pallas_call | solution.py:128
  206.5 21.4 %outer.5.into_ref = bf16[3072,4608]{1,0:T(8,128)(2,1)} custom-call(s32[4]{0:T(128)} %iota_xor_fusion.2.place.scalars, bf16[3072,1024]{1,0:T(8,128)(2,1)} %turn.2.left_ref, bf16[1024,2304]{1,0:T(8,128)(2,1)} %get-tuple-element.61.refs_0_), custom_call_target="tpu_custom_call" | custom-call | flops 14495514624 | bytes 14495514 | tf_op jit(solution)/shard_map/outer/pallas_call | solution.py:221
  228.1 3.5 collective-permute-done.12
  233.1 14.1 %collective-permute-start.13 = (bf16[1,128,3072]{2,1,0:T(8,128)(2,1)}, bf16[1,128,3072]{2,1,0:T(8,128)(2,1)}, u32[]{:S(2)}, u32[]{:S(2)}) collective-permute-start(bf16[1,128,3072]{2,1,0:T(8,128)(2,1)} %add_convert_fusion.1), channel_id=1, source_target_pairs={{0,2},{1,3},{2,0},{3,1},{4,6},{5,7},{6,4},{7,5},{8,10},{9,11},{10,... | collective-permute-start | bytes 2359304 | tf_op jit(solution)/shard_map/ppermute | solution.py:34
  247.2 15.2 %grad_terms.5 = (bf16[2,128,3072]{2,1,0:T(8,128)(2,1)}, f32[2,128,3072]{2,1,0:T(8,128)}, bf16[512,2304]{1,0:T(8,128)(2,1)}) custom-call(s32[4]{0:T(128)} %iota_xor_fusion.2.place.scalars, bf16[128,2304]{1,0:T(8,128)(2,1)} %collective-permute-done.8.refs_0_, bf16[128,2304]{1,0:T(8,128)(2,1)} %collective-permute-done.9.refs_1_, ...), custom_call_target="tpu_custom_call" | custom-call | flops 7247757312 | bytes 7247757 | tf_op jit(solution)/shard_map/grad_terms/pallas_call | solution.py:128
  262.4 3.0 collective-permute-done.13
  265.4 3.1 fusion.2
  269.9 2.2 add_convert_fusion
  272.1 1.7 collective-permute-start.16
  273.9 10.3 %outer.6.into_ref = bf16[3072,4608]{1,0:T(8,128)(2,1)} custom-call(s32[4]{0:T(128)} %iota_xor_fusion.2.place.scalars, bf16[3072,4608]{1,0:T(8,128)(2,1)} %outer.5.into_ref, bf16[3072,1024]{1,0:T(8,128)(2,1)} %turn.2.left_ref, bf16[512,2304]{1,0:T(8,128)(2,1)} %get-tuple-element.72.refs_0_, ...), custom_call_target="tpu_custom_call", output_to_operand_aliasing={{}: (1, {})} | custom-call | flops 4831838208 | bytes 4831838 | tf_op jit(solution)/shard_map/outer/pallas_call | solution.py:221
  284.1 10.3 %outer.7.into_ref = bf16[3072,4608]{1,0:T(8,128)(2,1)} custom-call(s32[4]{0:T(128)} %iota_xor_fusion.2.place.scalars, bf16[3072,4608]{1,0:T(8,128)(2,1)} %outer.6.into_ref, bf16[3072,1024]{1,0:T(8,128)(2,1)} %turn.2.left_ref, bf16[512,2304]{1,0:T(8,128)(2,1)} %get-tuple-element.72.refs_0_, ...), custom_call_target="tpu_custom_call", output_to_operand_aliasing={{}: (1, {})} | custom-call | flops 4831838208 | bytes 4831838 | tf_op jit(solution)/shard_map/outer/pallas_call | solution.py:221
  294.4 3.4 fusion
  297.9 2.2 collective-permute-start.17
  301.4 1.9 collective-permute-start.19
  303.3 10.3 %outer.8 = bf16[3072,4608]{1,0:T(8,128)(2,1)} custom-call(s32[4]{0:T(128)} %iota_xor_fusion.2.place.scalars, bf16[3072,4608]{1,0:T(8,128)(2,1)} %outer.7.into_ref, bf16[3072,1024]{1,0:T(8,128)(2,1)} %turn.2.left_ref, bf16[512,2304]{1,0:T(8,128)(2,1)} %get-tuple-element.72.refs_0_, ...), custom_call_target="tpu_custom_call", output_to_operand_aliasing={{}: (1, {})} | custom-call | flops 4831838208 | bytes 4831838 | tf_op jit(solution)/shard_map/outer/pallas_call | solution.py:221
  313.6 6.1 %collective-permute-done.17.refs_2_ = bf16[128,3072]{1,0:T(8,128)(2,1)} collective-permute-done((bf16[128,3072]{1,0:T(8,128)(2,1)}, bf16[128,3072]{1,0:T(8,128)(2,1)}, u32[]{:S(2)}, u32[]{:S(2)}) %collective-permute-start.17) | collective-permute-done | bytes 786464 | tf_op jit(solution)/shard_map/ppermute | solution.py:44
  319.7 2.2 collective-permute-done.18.refs_0_
  322.0 1.9 collective-permute-start.20
  324.5 3.4 collective-permute-start.21
  327.8 2.1 collective-permute-start.23
  330.0 3.6 broadcast_select_fusion.1
  333.6 12.2 %attn_terms.2 = (bf16[2,128,1536]{2,1,0:T(8,128)(2,1)}, f32[2,128,1536]{2,1,0:T(8,128)}, bf16[4,128,3072]{2,1,0:T(8,128)(2,1)}) custom-call(s32[9]{0:T(128)} %pad_add_fusion.scalars, bf16[128,3072]{1,0:T(8,128)(2,1)} %collective-permute-done.14.refs_0_, bf16[128,3072]{1,0:T(8,128)(2,1)} %collective-permute-done.19.refs_1_, ...), custom_call_target="tpu_custom_call" | custom-call | flops 4831838208 | bytes 4831838 | tf_op jit(solution)/shard_map/attn_terms/pallas_call | solution.py:173
  347.4 2.1 collective-permute-start.24
  349.5 3.7 fusion.1
  354.4 12.4 %attn_terms.3 = (bf16[2,128,1536]{2,1,0:T(8,128)(2,1)}, f32[2,128,1536]{2,1,0:T(8,128)}, bf16[4,128,3072]{2,1,0:T(8,128)(2,1)}) custom-call(s32[9]{0:T(128)} %pad_add_fusion.scalars, bf16[128,3072]{1,0:T(8,128)(2,1)} %collective-permute-done.18.refs_0_, bf16[128,3072]{1,0:T(8,128)(2,1)} %collective-permute-done.23.refs_1_, ...), custom_call_target="tpu_custom_call" | custom-call | flops 4831838208 | bytes 4831838 | tf_op jit(solution)/shard_map/attn_terms/pallas_call | solution.py:173
  366.8 1.8 add_convert_fusion.5
  369.9 15.1 %outer.9 = bf16[1536,3072]{1,0:T(8,128)(2,1)} custom-call(s32[4]{0:T(128)} %iota_xor_fusion.2.place.scalars, bf16[1536,1024]{1,0:T(8,128)(2,1)} %turn.3.left_ref, bf16[512,3072]{1,0:T(8,128)(2,1)} %bitcast.51, bf16[512,3072]{1,0:T(8,128)(2,1)} %bitcast.52), custom_call_target="tpu_custom_call" | custom-call | flops 9663676416 | bytes 9663676 | tf_op jit(solution)/shard_map/outer/pallas_call | solution.py:221
  385.0 11.1 %collective-permute-done.25 = bf16[1,128,1536]{2,1,0:T(8,128)(2,1)} collective-permute-done((bf16[1,128,1536]{2,1,0:T(8,128)(2,1)}, bf16[1,128,1536]{2,1,0:T(8,128)(2,1)}, u32[]{:S(2)}, u32[]{:S(2)}) %collective-permute-start.25) | collective-permute-done | bytes 393248 | tf_op jit(solution)/shard_map/ppermute | solution.py:34
  397.3 2.4 collective-permute-start.27
  400.9 15.6 %collective-permute-done.27 = bf16[1,128,1536]{2,1,0:T(8,128)(2,1)S(1)} collective-permute-done((bf16[1,128,1536]{2,1,0:T(8,128)(2,1)S(1)}, bf16[1,128,1536]{2,1,0:T(8,128)(2,1)S(1)}, u32[]{:S(2)}, u32[]{:S(2)}) %collective-permute-start.27) | collective-permute-done | bytes 393248 | tf_op jit(solution)/shard_map/ppermute | solution.py:34
  (60 shorter events, 16.6 us)
Async XLA Ops:
  2.0 31.5 %collective-permute-start = (bf16[256,2304]{1,0:T(8,128)(2,1)S(1)}, bf16[256,2304]{1,0:T(8,128)(2,1)}, u32[]{:S(2)}, u32[]{:S(2)}) collective-permute-start(bf16[256,2304]{1,0:T(8,128)(2,1)S(1)} %slice.77), channel_id=1, source_target_pairs={{0,0},{5,1},{10,2},{15,3},{1,4},{4,5},{11,6},{14,7},{2,8},{7,9},{8... | collective-permute-start | bytes 3538952 | tf_op jit(solution)/shard_map/ppermute | solution.py:56
  3.7 31.6 %collective-permute-start.1 = (bf16[256,2304]{1,0:T(8,128)(2,1)S(1)}, bf16[256,2304]{1,0:T(8,128)(2,1)}, u32[]{:S(2)}, u32[]{:S(2)}) collective-permute-start(bf16[256,2304]{1,0:T(8,128)(2,1)S(1)} %slice.77), channel_id=1, source_target_pairs={{1,0},{4,1},{11,2},{14,3},{0,4},{5,5},{10,6},{15,7},{3,8},{6,9},{9... | collective-permute-start | bytes 3538952 | tf_op jit(solution)/shard_map/ppermute | solution.py:56
  8.9 56.6 %collective-permute-start.2 = (bf16[256,2304]{1,0:T(8,128)(2,1)S(1)}, bf16[256,2304]{1,0:T(8,128)(2,1)}, u32[]{:S(2)}, u32[]{:S(2)}) collective-permute-start(bf16[256,2304]{1,0:T(8,128)(2,1)S(1)} %slice.77), channel_id=1, source_target_pairs={{2,0},{7,1},{8,2},{13,3},{3,4},{6,5},{9,6},{12,7},{0,8},{5,9},{10,... | collective-permute-start | bytes 3538952 | tf_op jit(solution)/shard_map/ppermute | solution.py:56
  14.3 69.0 %collective-permute-start.3 = (bf16[256,2304]{1,0:T(8,128)(2,1)S(1)}, bf16[256,2304]{1,0:T(8,128)(2,1)}, u32[]{:S(2)}, u32[]{:S(2)}) collective-permute-start(bf16[256,2304]{1,0:T(8,128)(2,1)S(1)} %slice.77), channel_id=1, source_target_pairs={{3,0},{6,1},{9,2},{12,3},{2,4},{7,5},{8,6},{13,7},{1,8},{4,9},{11,... | collective-permute-start | bytes 3538952 | tf_op jit(solution)/shard_map/ppermute | solution.py:56
  26.6 6.0 %copy-start.3 = (bf16[1,256,4608]{2,1,0:T(8,128)(2,1)S(1)}, bf16[1,256,4608]{2,1,0:T(8,128)(2,1)}, u32[]{:S(2)}) copy-start(bf16[1,256,4608]{2,1,0:T(8,128)(2,1)} %param.7) | copy-start | bytes 7077892
  83.3 69.8 %collective-permute-start.4 = (bf16[128,2304]{1,0:T(8,128)(2,1)S(1)}, bf16[128,2304]{1,0:T(8,128)(2,1)S(1)}, u32[]{:S(2)}, u32[]{:S(2)}) collective-permute-start(bf16[128,2304]{1,0:T(8,128)(2,1)S(1)} %get-tuple-element.53), channel_id=1, source_target_pairs={{0,0},{5,1},{10,2},{15,3},{1,4},{4,5},{11,6},{14,7},{2,8},{7,9},{8... | collective-permute-start | bytes 1769480 | tf_op jit(solution)/shard_map/ppermute | solution.py:56
  84.0 69.1 %collective-permute-start.5 = (bf16[128,2304]{1,0:T(8,128)(2,1)S(1)}, bf16[128,2304]{1,0:T(8,128)(2,1)S(1)}, u32[]{:S(2)}, u32[]{:S(2)}) collective-permute-start(bf16[128,2304]{1,0:T(8,128)(2,1)S(1)} %get-tuple-element.53), channel_id=1, source_target_pairs={{1,0},{4,1},{11,2},{14,3},{0,4},{5,5},{10,6},{15,7},{3,8},{6,9},{9... | collective-permute-start | bytes 1769480 | tf_op jit(solution)/shard_map/ppermute | solution.py:56
  120.1 33.0 %collective-permute-start.6 = (bf16[128,2304]{1,0:T(8,128)(2,1)S(1)}, bf16[128,2304]{1,0:T(8,128)(2,1)S(1)}, u32[]{:S(2)}, u32[]{:S(2)}) collective-permute-start(bf16[128,2304]{1,0:T(8,128)(2,1)S(1)} %get-tuple-element.53), channel_id=1, source_target_pairs={{2,0},{7,1},{8,2},{13,3},{3,4},{6,5},{9,6},{12,7},{0,8},{5,9},{10,... | collective-permute-start | bytes 1769480 | tf_op jit(solution)/shard_map/ppermute | solution.py:56
  124.3 32.3 %collective-permute-start.7 = (bf16[128,2304]{1,0:T(8,128)(2,1)S(1)}, bf16[128,2304]{1,0:T(8,128)(2,1)S(1)}, u32[]{:S(2)}, u32[]{:S(2)}) collective-permute-start(bf16[128,2304]{1,0:T(8,128)(2,1)S(1)} %get-tuple-element.53), channel_id=1, source_target_pairs={{3,0},{6,1},{9,2},{12,3},{2,4},{7,5},{8,6},{13,7},{1,8},{4,9},{11,... | collective-permute-start | bytes 1769480 | tf_op jit(solution)/shard_map/ppermute | solution.py:56
  153.1 38.2 %copy-start.6 = (bf16[128,2304]{1,0:T(8,128)(2,1)}, bf16[128,2304]{1,0:T(8,128)(2,1)S(1)}, u32[]{:S(2)}) copy-start(bf16[128,2304]{1,0:T(8,128)(2,1)S(1)} %collective-permute-done.4.refs_0_) | copy-start | bytes 1769476
  153.1 38.2 %copy-start.7 = (bf16[128,2304]{1,0:T(8,128)(2,1)}, bf16[128,2304]{1,0:T(8,128)(2,1)S(1)}, u32[]{:S(2)}) copy-start(bf16[128,2304]{1,0:T(8,128)(2,1)S(1)} %collective-permute-done.5.refs_1_) | copy-start | bytes 1769476
  153.1 38.2 %copy-start.8 = (bf16[128,2304]{1,0:T(8,128)(2,1)}, bf16[128,2304]{1,0:T(8,128)(2,1)S(1)}, u32[]{:S(2)}) copy-start(bf16[128,2304]{1,0:T(8,128)(2,1)S(1)} %collective-permute-done.6.refs_2_) | copy-start | bytes 1769476
  156.6 34.8 %copy-start.9 = (bf16[128,2304]{1,0:T(8,128)(2,1)}, bf16[128,2304]{1,0:T(8,128)(2,1)S(1)}, u32[]{:S(2)}) copy-start(bf16[128,2304]{1,0:T(8,128)(2,1)S(1)} %collective-permute-done.7.refs_3_) | copy-start | bytes 1769476
  156.6 71.4 %collective-permute-start.8 = (bf16[128,2304]{1,0:T(8,128)(2,1)}, bf16[128,2304]{1,0:T(8,128)(2,1)}, u32[]{:S(2)}, u32[]{:S(2)}) collective-permute-start(bf16[128,2304]{1,0:T(8,128)(2,1)} %get-tuple-element.59), channel_id=1, source_target_pairs={{0,0},{5,1},{10,2},{15,3},{1,4},{4,5},{11,6},{14,7},{2,8},{7,9},{8... | collective-permute-start | bytes 1769480 | tf_op jit(solution)/shard_map/ppermute | solution.py:56
  162.5 65.4 %collective-permute-start.9 = (bf16[128,2304]{1,0:T(8,128)(2,1)}, bf16[128,2304]{1,0:T(8,128)(2,1)}, u32[]{:S(2)}, u32[]{:S(2)}) collective-permute-start(bf16[128,2304]{1,0:T(8,128)(2,1)} %get-tuple-element.59), channel_id=1, source_target_pairs={{1,0},{4,1},{11,2},{14,3},{0,4},{5,5},{10,6},{15,7},{3,8},{6,9},{9... | collective-permute-start | bytes 1769480 | tf_op jit(solution)/shard_map/ppermute | solution.py:56
  180.5 47.5 %collective-permute-start.10 = (bf16[128,2304]{1,0:T(8,128)(2,1)}, bf16[128,2304]{1,0:T(8,128)(2,1)}, u32[]{:S(2)}, u32[]{:S(2)}) collective-permute-start(bf16[128,2304]{1,0:T(8,128)(2,1)} %get-tuple-element.59), channel_id=1, source_target_pairs={{2,0},{7,1},{8,2},{13,3},{3,4},{6,5},{9,6},{12,7},{0,8},{5,9},{10,... | collective-permute-start | bytes 1769480 | tf_op jit(solution)/shard_map/ppermute | solution.py:56
  184.8 43.1 %collective-permute-start.11 = (bf16[128,2304]{1,0:T(8,128)(2,1)}, bf16[128,2304]{1,0:T(8,128)(2,1)}, u32[]{:S(2)}, u32[]{:S(2)}) collective-permute-start(bf16[128,2304]{1,0:T(8,128)(2,1)} %get-tuple-element.59), channel_id=1, source_target_pairs={{3,0},{6,1},{9,2},{12,3},{2,4},{7,5},{8,6},{13,7},{1,8},{4,9},{11,... | collective-permute-start | bytes 1769480 | tf_op jit(solution)/shard_map/ppermute | solution.py:56
  206.5 25.1 %copy-start = (f32[2,128,3072]{2,1,0:T(8,128)S(1)}, f32[2,128,3072]{2,1,0:T(8,128)}, u32[]{:S(2)}) copy-start(f32[2,128,3072]{2,1,0:T(8,128)} %get-tuple-element.57) | copy-start | bytes 9437188
  228.0 3.7 collective-permute-start.12
  231.6 1.4 copy-start.2
  233.1 32.3 %collective-permute-start.13 = (bf16[1,128,3072]{2,1,0:T(8,128)(2,1)}, bf16[1,128,3072]{2,1,0:T(8,128)(2,1)}, u32[]{:S(2)}, u32[]{:S(2)}) collective-permute-start(bf16[1,128,3072]{2,1,0:T(8,128)(2,1)} %add_convert_fusion.1), channel_id=1, source_target_pairs={{0,2},{1,3},{2,0},{3,1},{4,6},{5,7},{6,4},{7,5},{8,10},{9,11},{10,... | collective-permute-start | bytes 2359304 | tf_op jit(solution)/shard_map/ppermute | solution.py:34
  265.4 4.5 %collective-permute-start.15 = (bf16[2,128,3072]{2,1,0:T(8,128)(2,1)}, bf16[2,128,3072]{2,1,0:T(8,128)(2,1)}, u32[]{:S(2)}, u32[]{:S(2)}) collective-permute-start(bf16[2,128,3072]{2,1,0:T(8,128)(2,1)} %get-tuple-element.69), channel_id=1, source_target_pairs={{0,1},{1,0},{2,3},{3,2},{4,5},{5,4},{6,7},{7,6},{8,9},{9,8},{10,11... | collective-permute-start | bytes 4718600 | tf_op jit(solution)/shard_map/ppermute | solution.py:34
  265.4 4.5 %copy-start.1 = (f32[2,128,3072]{2,1,0:T(8,128)S(1)}, f32[2,128,3072]{2,1,0:T(8,128)}, u32[]{:S(2)}) copy-start(f32[2,128,3072]{2,1,0:T(8,128)} %get-tuple-element.68) | copy-start | bytes 9437188
  268.4 26.0 %collective-permute-start.14 = (bf16[128,3072]{1,0:T(8,128)(2,1)}, bf16[128,3072]{1,0:T(8,128)(2,1)}, u32[]{:S(2)}, u32[]{:S(2)}) collective-permute-start(bf16[128,3072]{1,0:T(8,128)(2,1)} %fusion.2), channel_id=1, source_target_pairs={{16,0},{17,1},{18,2},{19,3},{20,4},{21,5},{22,6},{23,7},{24,8},{25... | collective-permute-start | bytes 2359304 | tf_op jit(solution)/shard_map/ppermute | solution.py:50
  272.1 22.3 %collective-permute-start.16 = (bf16[1,128,3072]{2,1,0:T(8,128)(2,1)}, bf16[1,128,3072]{2,1,0:T(8,128)(2,1)}, u32[]{:S(2)}, u32[]{:S(2)}) collective-permute-start(bf16[1,128,3072]{2,1,0:T(8,128)(2,1)} %add_convert_fusion), channel_id=1, source_target_pairs={{0,2},{1,3},{2,0},{3,1},{4,6},{5,7},{6,4},{7,5},{8,10},{9,11},{10,... | collective-permute-start | bytes 2359304 | tf_op jit(solution)/shard_map/ppermute | solution.py:34
  297.9 21.9 %collective-permute-start.17 = (bf16[128,3072]{1,0:T(8,128)(2,1)}, bf16[128,3072]{1,0:T(8,128)(2,1)}, u32[]{:S(2)}, u32[]{:S(2)}) collective-permute-start(bf16[128,3072]{1,0:T(8,128)(2,1)} %collective-permute-done.14.refs_0_), channel_id=1, source_target_pairs={{0,2},{1,3},{2,0},{3,1},{4,6},{5,7},{6,4},{7,5},{8,10},{9,11},{10,... | collective-permute-start | bytes 2359304 | tf_op jit(solution)/shard_map/ppermute | solution.py:44
  300.1 21.9 %collective-permute-start.18 = (bf16[128,3072]{1,0:T(8,128)(2,1)}, bf16[128,3072]{1,0:T(8,128)(2,1)}, u32[]{:S(2)}, u32[]{:S(2)}) collective-permute-start(bf16[128,3072]{1,0:T(8,128)(2,1)} %fusion), channel_id=1, source_target_pairs={{16,0},{17,1},{18,2},{19,3},{20,4},{21,5},{22,6},{23,7},{24,8},{25... | collective-permute-start | bytes 2359304 | tf_op jit(solution)/shard_map/ppermute | solution.py:50
  301.4 22.5 %copy-start.10 = (s32[4]{0:T(128)S(1)}, s32[4]{0:T(128)}, u32[]{:S(2)}) copy-start(s32[4]{0:T(128)} %iota_xor_fusion.1.token) | copy-start | bytes 52
  301.4 32.2 %collective-permute-start.19 = (bf16[128,3072]{1,0:T(8,128)(2,1)}, bf16[128,3072]{1,0:T(8,128)(2,1)}, u32[]{:S(2)}, u32[]{:S(2)}) collective-permute-start(bf16[128,3072]{1,0:T(8,128)(2,1)} %collective-permute-done.14.refs_0_), channel_id=1, source_target_pairs={{0,1},{1,0},{2,3},{3,2},{4,5},{5,4},{6,7},{7,6},{8,9},{9,8},{10,11... | collective-permute-start | bytes 2359304 | tf_op jit(solution)/shard_map/ppermute | solution.py:44
  322.0 11.7 %collective-permute-start.20 = (bf16[128,3072]{1,0:T(8,128)(2,1)}, bf16[128,3072]{1,0:T(8,128)(2,1)}, u32[]{:S(2)}, u32[]{:S(2)}) collective-permute-start(bf16[128,3072]{1,0:T(8,128)(2,1)} %collective-permute-done.17.refs_2_), channel_id=1, source_target_pairs={{0,1},{1,0},{2,3},{3,2},{4,5},{5,4},{6,7},{7,6},{8,9},{9,8},{10,11... | collective-permute-start | bytes 2359304 | tf_op jit(solution)/shard_map/ppermute | solution.py:44
  324.5 22.1 %collective-permute-start.21 = (bf16[128,3072]{1,0:T(8,128)(2,1)}, bf16[128,3072]{1,0:T(8,128)(2,1)}, u32[]{:S(2)}, u32[]{:S(2)}) collective-permute-start(bf16[128,3072]{1,0:T(8,128)(2,1)} %collective-permute-done.18.refs_0_), channel_id=1, source_target_pairs={{0,2},{1,3},{2,0},{3,1},{4,6},{5,7},{6,4},{7,5},{8,10},{9,11},{10,... | collective-permute-start | bytes 2359304 | tf_op jit(solution)/shard_map/ppermute | solution.py:44
  327.8 26.6 %collective-permute-start.23 = (bf16[128,3072]{1,0:T(8,128)(2,1)}, bf16[128,3072]{1,0:T(8,128)(2,1)}, u32[]{:S(2)}, u32[]{:S(2)}) collective-permute-start(bf16[128,3072]{1,0:T(8,128)(2,1)} %collective-permute-done.18.refs_0_), channel_id=1, source_target_pairs={{0,1},{1,0},{2,3},{3,2},{4,5},{5,4},{6,7},{7,6},{8,9},{9,8},{10,11... | collective-permute-start | bytes 2359304 | tf_op jit(solution)/shard_map/ppermute | solution.py:44
  346.6 20.2 %collective-permute-start.22 = (bf16[2,128,1536]{2,1,0:T(8,128)(2,1)}, bf16[2,128,1536]{2,1,0:T(8,128)(2,1)}, u32[]{:S(2)}, u32[]{:S(2)}) collective-permute-start(bf16[2,128,1536]{2,1,0:T(8,128)(2,1)} %get-tuple-element.83), channel_id=1, source_target_pairs={{0,4},{4,0},{8,12},{12,8},{1,5},{5,1},{9,13},{13,9},{2,6},{6,2},{1... | collective-permute-start | bytes 2359304 | tf_op jit(solution)/shard_map/ppermute | solution.py:34
  347.4 7.1 %collective-permute-start.24 = (bf16[128,3072]{1,0:T(8,128)(2,1)}, bf16[128,3072]{1,0:T(8,128)(2,1)}, u32[]{:S(2)}, u32[]{:S(2)}) collective-permute-start(bf16[128,3072]{1,0:T(8,128)(2,1)} %collective-permute-done.21.refs_2_), channel_id=1, source_target_pairs={{0,1},{1,0},{2,3},{3,2},{4,5},{5,4},{6,7},{7,6},{8,9},{9,8},{10,11... | collective-permute-start | bytes 2359304 | tf_op jit(solution)/shard_map/ppermute | solution.py:44
  354.4 12.4 %copy-start.4 = (f32[2,128,1536]{2,1,0:T(8,128)S(1)}, f32[2,128,1536]{2,1,0:T(8,128)}, u32[]{:S(2)}) copy-start(f32[2,128,1536]{2,1,0:T(8,128)} %get-tuple-element.87) | copy-start | bytes 4718596
  368.6 28.6 %collective-permute-start.26 = (bf16[2,128,1536]{2,1,0:T(8,128)(2,1)}, bf16[2,128,1536]{2,1,0:T(8,128)(2,1)S(1)}, u32[]{:S(2)}, u32[]{:S(2)}) collective-permute-start(bf16[2,128,1536]{2,1,0:T(8,128)(2,1)} %get-tuple-element.93), channel_id=1, source_target_pairs={{0,4},{4,0},{8,12},{12,8},{1,5},{5,1},{9,13},{13,9},{2,6},{6,2},{1... | collective-permute-start | bytes 2359304 | tf_op jit(solution)/shard_map/ppermute | solution.py:34
  369.9 26.2 %collective-permute-start.25 = (bf16[1,128,1536]{2,1,0:T(8,128)(2,1)}, bf16[1,128,1536]{2,1,0:T(8,128)(2,1)}, u32[]{:S(2)}, u32[]{:S(2)}) collective-permute-start(bf16[1,128,1536]{2,1,0:T(8,128)(2,1)} %add_convert_fusion.5), channel_id=1, source_target_pairs={{0,8},{4,12},{8,0},{12,4},{1,9},{5,13},{9,1},{13,5},{2,10},{6,14},... | collective-permute-start | bytes 1179656 | tf_op jit(solution)/shard_map/ppermute | solution.py:34
  369.9 27.3 %copy-start.5 = (f32[2,128,1536]{2,1,0:T(8,128)S(1)}, f32[2,128,1536]{2,1,0:T(8,128)}, u32[]{:S(2)}) copy-start(f32[2,128,1536]{2,1,0:T(8,128)} %get-tuple-element.95) | copy-start | bytes 4718596
  397.3 19.2 %collective-permute-start.27 = (bf16[1,128,1536]{2,1,0:T(8,128)(2,1)S(1)}, bf16[1,128,1536]{2,1,0:T(8,128)(2,1)S(1)}, u32[]{:S(2)}, u32[]{:S(2)}) collective-permute-start(bf16[1,128,1536]{2,1,0:T(8,128)(2,1)S(1)} %add_convert_fusion.3), channel_id=1, source_target_pairs={{0,8},{4,12},{8,0},{12,4},{1,9},{5,13},{9,1},{13,5},{2,10},{6,14},... | collective-permute-start | bytes 1179656 | tf_op jit(solution)/shard_map/ppermute | solution.py:34

commit v3 on v2

--- a/solution.py
+++ b/solution.py
@@ -337,7 +337,7 @@
             if bit > 1:
                 yield [], list(got.values())
                 got = {d: slots.gate(block) for d, block in got.items()}
-                have["lower", q] = (slots.gate(upper).astype(F32) + down).astype(BF16)
+                have["lower", q] = upper, down
             below.update(got)
         have["upper", q] = [below[d] for d in range(n)]
 
@@ -454,17 +454,26 @@
             return [spare.pop(0) for _ in spare[: max(1, len(spare) - 1)]]
         if attns:
             return []
+        if not spare and not outs:
+            return [ends.pop()] if ends else []
         final = spare + outs
         spare.clear()
         outs.clear()
         return final
 
+    def lowers():
+        parts = [have["lower", q] for q in range(len(spans))]
+        parts = [(slots.gate(upper).astype(F32) + down).astype(BF16) for upper, down in parts]
+        have["lowers"] = jnp.concatenate(parts, axis=0)
+        return have["lowers"]
+
+    ends = [lowers]
     slots.tasks.append(gather())
     slots.run(lambda: [turn("inputs", qkv_input[0]), turn("attn_out", attn_out[0])])
     for piece in range(last_piece):
         both = piece < last_piece - 1
         slots.run(lambda: [early_terms(piece)] + [early_grad(piece)] * both)
-    while slots.tasks or terms or attns or spare or outs:
+    while slots.tasks or terms or attns or spare or outs or ends:
         slots.run(late)
 
     every = range(len(spans))
@@ -472,7 +481,7 @@
         have["grad"][None],
         have["out"][None],
         jnp.concatenate([have["attn", q] for q in every], axis=0)[None],
-        jnp.concatenate([have["lower", q] for q in every], axis=0)[None],
+        have["lowers"][None],
     )
 
 

time: 419 us -> 424 us (1.012)
  transfers between devices with their start and end apart: 28 -> 28, of which waited for: 12 -> 12; matrix products, arithmetic and copies ran while one was open for 4% -> 4% of each run, Pallas kernels for 38% -> 37%
where the time goes in v3:
time: 424 us; the launch traced here: 422 us
  Pallas kernels  157 us (37%)
  starting transfers between devices  138 us (33%)
  waiting for transfers between devices  97.9 us (23%)
  other arithmetic  24.6 us (6%)
    ppermute x12, starting transfers between devices, direct(): return lax.ppermute(block, ('row', 'col'), route)  102 us
    pallas_call x5, Pallas kernels, outer(): pl.pallas_call(functools.partial(kernel, order), out_shape=shape((left.sh...  67.3 us
    pallas_call x3, Pallas kernels, grad_terms(): pl.pallas_call(functools.partial(terms_kernel, n, more, split), out_shape...  52.6 us
    ppermute x12, waiting for transfers between devices, direct(): return lax.ppermute(block, ('row', 'col'), route)  51 us
    ppermute x8, waiting for transfers between devices, swap(): return lax.ppermute(block, axis, route)  34.6 us
    pallas_call x2, Pallas kernels, attn_terms(): pl.pallas_call(functools.partial(attn_kernel, n), out_shape=[shape(half,...  24.3 us
    ppermute x8, starting transfers between devices, swap(): return lax.ppermute(block, axis, route)  19.3 us
    ppermute x6, starting transfers between devices, swap_below(): return lax.ppermute(block, ('section', 'col'), route)  13.7 us
  transfers between devices with their start and end apart: 28, of which 12 were waited for; matrix products, arithmetic and copies ran while one was open for 4% of the time, Pallas kernels for 37%

profile of v3, /device:TPU:0, one launch (start us, length us, event | category | flops | bytes accessed | tf_op | source)
XLA Modules:
  0.0 422.0 jit_solution(11163156643091667676)
XLA Ops:
  0.6 2.4 slice.77
  3.0 10.4 %collective-permute-start = (bf16[256,2304]{1,0:T(8,128)(2,1)}, bf16[256,2304]{1,0:T(8,128)(2,1)}, u32[]{:S(2)}, u32[]{:S(2)}) collective-permute-start(bf16[256,2304]{1,0:T(8,128)(2,1)} %slice.77), channel_id=1, source_target_pairs={{0,0},{5,1},{10,2},{15,3},{1,4},{4,5},{11,6},{14,7},{2,8},{7,9},{8... | collective-permute-start | bytes 3538952 | tf_op jit(solution)/shard_map/ppermute | solution.py:56
  13.4 1.9 collective-permute-start.1
  15.3 1.9 collective-permute-start.2
  17.2 2.6 collective-permute-start.3
  20.3 7.2 %turn.2.left_ref = bf16[3072,1024]{1,0:T(8,128)(2,1)} custom-call(s32[4]{0:T(128)} %iota_xor_fusion.1.token, bf16[1024,3072]{1,0:T(8,128)(2,1)} %bitcast.47), custom_call_target="tpu_custom_call" | custom-call | flops 25165824 | bytes 25165 | tf_op jit(solution)/shard_map/turn/pallas_call | solution.py:74
  27.5 5.5 %turn.3.left_ref = bf16[1536,1024]{1,0:T(8,128)(2,1)} custom-call(s32[4]{0:T(128)} %iota_xor_fusion.1.token, bf16[1024,1536]{1,0:T(8,128)(2,1)} %bitcast.48), custom_call_target="tpu_custom_call" | custom-call | flops 12582912 | bytes 12582 | tf_op jit(solution)/shard_map/turn/pallas_call | solution.py:74
  33.7 8.4 %collective-permute-done.1.refs_1_ = bf16[256,2304]{1,0:T(8,128)(2,1)} collective-permute-done((bf16[256,2304]{1,0:T(8,128)(2,1)}, bf16[256,2304]{1,0:T(8,128)(2,1)}, u32[]{:S(2)}, u32[]{:S(2)}) %collective-permute-start.1) | collective-permute-done | bytes 1179680 | tf_op jit(solution)/shard_map/ppermute | solution.py:56
  42.0 28.0 %collective-permute-done.2.refs_2_ = bf16[256,2304]{1,0:T(8,128)(2,1)} collective-permute-done((bf16[256,2304]{1,0:T(8,128)(2,1)}, bf16[256,2304]{1,0:T(8,128)(2,1)}, u32[]{:S(2)}, u32[]{:S(2)}) %collective-permute-start.2) | collective-permute-done | bytes 1179680 | tf_op jit(solution)/shard_map/ppermute | solution.py:56
  70.0 14.6 %collective-permute-done.3.refs_3_ = bf16[256,2304]{1,0:T(8,128)(2,1)} collective-permute-done((bf16[256,2304]{1,0:T(8,128)(2,1)}, bf16[256,2304]{1,0:T(8,128)(2,1)}, u32[]{:S(2)}, u32[]{:S(2)}) %collective-permute-start.3) | collective-permute-done | bytes 1179680 | tf_op jit(solution)/shard_map/ppermute | solution.py:56
  85.3 36.2 %collective-permute-start.5 = (bf16[128,2304]{1,0:T(8,128)(2,1)S(1)}, bf16[128,2304]{1,0:T(8,128)(2,1)S(1)}, u32[]{:S(2)}, u32[]{:S(2)}) collective-permute-start(bf16[128,2304]{1,0:T(8,128)(2,1)S(1)} %get-tuple-element.54), channel_id=1, source_target_pairs={{1,0},{4,1},{11,2},{14,3},{0,4},{5,5},{10,6},{15,7},{3,8},{6,9},{9... | collective-permute-start | bytes 1769480 | tf_op jit(solution)/shard_map/ppermute | solution.py:56
  121.5 4.1 collective-permute-start.6
  125.6 6.5 %collective-permute-start.7 = (bf16[128,2304]{1,0:T(8,128)(2,1)S(1)}, bf16[128,2304]{1,0:T(8,128)(2,1)S(1)}, u32[]{:S(2)}, u32[]{:S(2)}) collective-permute-start(bf16[128,2304]{1,0:T(8,128)(2,1)S(1)} %get-tuple-element.54), channel_id=1, source_target_pairs={{3,0},{6,1},{9,2},{12,3},{2,4},{7,5},{8,6},{13,7},{1,8},{4,9},{11,... | collective-permute-start | bytes 1769480 | tf_op jit(solution)/shard_map/ppermute | solution.py:56
  132.1 22.2 %grad_terms.3 = (f32[4,256,3072]{2,1,0:T(8,128)}, bf16[1024,2304]{1,0:T(8,128)(2,1)}) custom-call(s32[4]{0:T(128)} %iota_xor_fusion.2.place.scalars, bf16[256,2304]{1,0:T(8,128)(2,1)} %collective-permute-done.refs_0_, bf16[256,2304]{1,0:T(8,128)(2,1)} %collective-permute-done.1.refs_1_, bf16[256,2304]{1,0:T(8,128)(2,1)} %collective-permute-done.2.refs_2_, ...), custom_call_target="tpu_custom_call" | custom-call | flops 14495514624 | bytes 14495514 | tf_op jit(solution)/shard_map/grad_terms/pallas_call | solution.py:128
  155.9 25.9 %collective-permute-start.9 = (bf16[128,2304]{1,0:T(8,128)(2,1)S(1)}, bf16[128,2304]{1,0:T(8,128)(2,1)}, u32[]{:S(2)}, u32[]{:S(2)}) collective-permute-start(bf16[128,2304]{1,0:T(8,128)(2,1)S(1)} %get-tuple-element.60), channel_id=1, source_target_pairs={{1,0},{4,1},{11,2},{14,3},{0,4},{5,5},{10,6},{15,7},{3,8},{6,9},{9... | collective-permute-start | bytes 1769480 | tf_op jit(solution)/shard_map/ppermute | solution.py:56
  181.8 4.3 %collective-permute-start.10 = (bf16[128,2304]{1,0:T(8,128)(2,1)S(1)}, bf16[128,2304]{1,0:T(8,128)(2,1)}, u32[]{:S(2)}, u32[]{:S(2)}) collective-permute-start(bf16[128,2304]{1,0:T(8,128)(2,1)S(1)} %get-tuple-element.60), channel_id=1, source_target_pairs={{2,0},{7,1},{8,2},{13,3},{3,4},{6,5},{9,6},{12,7},{0,8},{5,9},{10,... | collective-permute-start | bytes 1769480 | tf_op jit(solution)/shard_map/ppermute | solution.py:56
  186.0 6.5 %collective-permute-start.11 = (bf16[128,2304]{1,0:T(8,128)(2,1)S(1)}, bf16[128,2304]{1,0:T(8,128)(2,1)}, u32[]{:S(2)}, u32[]{:S(2)}) collective-permute-start(bf16[128,2304]{1,0:T(8,128)(2,1)S(1)} %get-tuple-element.60), channel_id=1, source_target_pairs={{3,0},{6,1},{9,2},{12,3},{2,4},{7,5},{8,6},{13,7},{1,8},{4,9},{11,... | collective-permute-start | bytes 1769480 | tf_op jit(solution)/shard_map/ppermute | solution.py:56
  192.6 15.2 %grad_terms.4 = (bf16[2,128,3072]{2,1,0:T(8,128)(2,1)}, f32[2,128,3072]{2,1,0:T(8,128)}, bf16[512,2304]{1,0:T(8,128)(2,1)}) custom-call(s32[4]{0:T(128)} %iota_xor_fusion.2.place.scalars, bf16[128,2304]{1,0:T(8,128)(2,1)} %copy-done.11, bf16[128,2304]{1,0:T(8,128)(2,1)} %copy-done.12, bf16[128,2304]{1,0:T(8,128)(2,1)} %copy-done.13, ...), custom_call_target="tpu_custom_call" | custom-call | flops 7247757312 | bytes 7247757 | tf_op jit(solution)/shard_map/grad_terms/pallas_call | solution.py:128
  207.8 21.4 %outer.5.into_ref = bf16[3072,4608]{1,0:T(8,128)(2,1)} custom-call(s32[4]{0:T(128)} %iota_xor_fusion.2.place.scalars, bf16[3072,1024]{1,0:T(8,128)(2,1)} %turn.2.left_ref, bf16[1024,2304]{1,0:T(8,128)(2,1)} %get-tuple-element.62.refs_0_), custom_call_target="tpu_custom_call" | custom-call | flops 14495514624 | bytes 14495514 | tf_op jit(solution)/shard_map/outer/pallas_call | solution.py:221
  229.4 3.5 collective-permute-done.12
  234.0 13.7 %collective-permute-start.13 = (bf16[1,128,3072]{2,1,0:T(8,128)(2,1)S(1)}, bf16[1,128,3072]{2,1,0:T(8,128)(2,1)}, u32[]{:S(2)}, u32[]{:S(2)}) collective-permute-start(bf16[1,128,3072]{2,1,0:T(8,128)(2,1)S(1)} %add_convert_fusion.1), channel_id=1, source_target_pairs={{0,2},{1,3},{2,0},{3,1},{4,6},{5,7},{6,4},{7,5},{8,10},{9,11},{10,... | collective-permute-start | bytes 2359304 | tf_op jit(solution)/shard_map/ppermute | solution.py:34
  247.7 15.2 %grad_terms.5 = (bf16[2,128,3072]{2,1,0:T(8,128)(2,1)}, f32[2,128,3072]{2,1,0:T(8,128)}, bf16[512,2304]{1,0:T(8,128)(2,1)}) custom-call(s32[4]{0:T(128)} %iota_xor_fusion.2.place.scalars, bf16[128,2304]{1,0:T(8,128)(2,1)} %collective-permute-done.8.refs_0_, bf16[128,2304]{1,0:T(8,128)(2,1)} %collective-permute-done.9.refs_1_, ...), custom_call_target="tpu_custom_call" | custom-call | flops 7247757312 | bytes 7247757 | tf_op jit(solution)/shard_map/grad_terms/pallas_call | solution.py:128
  262.9 2.8 collective-permute-done.13
  265.6 3.1 fusion.2
  270.2 2.2 add_convert_fusion
  274.1 10.3 %outer.6.into_ref = bf16[3072,4608]{1,0:T(8,128)(2,1)} custom-call(s32[4]{0:T(128)} %iota_xor_fusion.2.place.scalars, bf16[3072,4608]{1,0:T(8,128)(2,1)} %outer.5.into_ref, bf16[3072,1024]{1,0:T(8,128)(2,1)} %turn.2.left_ref, bf16[512,2304]{1,0:T(8,128)(2,1)} %get-tuple-element.73.refs_0_, ...), custom_call_target="tpu_custom_call", output_to_operand_aliasing={{}: (1, {})} | custom-call | flops 4831838208 | bytes 4831838 | tf_op jit(solution)/shard_map/outer/pallas_call | solution.py:221
  284.4 10.3 %outer.7.into_ref = bf16[3072,4608]{1,0:T(8,128)(2,1)} custom-call(s32[4]{0:T(128)} %iota_xor_fusion.2.place.scalars, bf16[3072,4608]{1,0:T(8,128)(2,1)} %outer.6.into_ref, bf16[3072,1024]{1,0:T(8,128)(2,1)} %turn.2.left_ref, bf16[512,2304]{1,0:T(8,128)(2,1)} %get-tuple-element.73.refs_0_, ...), custom_call_target="tpu_custom_call", output_to_operand_aliasing={{}: (1, {})} | custom-call | flops 4831838208 | bytes 4831838 | tf_op jit(solution)/shard_map/outer/pallas_call | solution.py:221
  294.7 3.5 fusion
  298.2 2.3 collective-permute-start.17
  301.8 1.9 collective-permute-start.19
  303.7 10.3 %outer.8 = bf16[3072,4608]{1,0:T(8,128)(2,1)} custom-call(s32[4]{0:T(128)} %iota_xor_fusion.2.place.scalars, bf16[3072,4608]{1,0:T(8,128)(2,1)} %outer.7.into_ref, bf16[3072,1024]{1,0:T(8,128)(2,1)} %turn.2.left_ref, bf16[512,2304]{1,0:T(8,128)(2,1)} %get-tuple-element.73.refs_0_, ...), custom_call_target="tpu_custom_call", output_to_operand_aliasing={{}: (1, {})} | custom-call | flops 4831838208 | bytes 4831838 | tf_op jit(solution)/shard_map/outer/pallas_call | solution.py:221
  314.0 6.2 %collective-permute-done.17.refs_2_ = bf16[128,3072]{1,0:T(8,128)(2,1)} collective-permute-done((bf16[128,3072]{1,0:T(8,128)(2,1)}, bf16[128,3072]{1,0:T(8,128)(2,1)}, u32[]{:S(2)}, u32[]{:S(2)}) %collective-permute-start.17) | collective-permute-done | bytes 786464 | tf_op jit(solution)/shard_map/ppermute | solution.py:44
  320.2 2.2 collective-permute-done.18.refs_0_
  322.4 1.9 collective-permute-start.20
  324.4 3.3 collective-permute-start.21
  328.3 2.1 collective-permute-start.23
  330.5 12.2 %attn_terms.2 = (bf16[2,128,1536]{2,1,0:T(8,128)(2,1)}, f32[2,128,1536]{2,1,0:T(8,128)}, bf16[4,128,3072]{2,1,0:T(8,128)(2,1)}) custom-call(s32[9]{0:T(128)} %pad_add_fusion.scalars, bf16[128,3072]{1,0:T(8,128)(2,1)} %collective-permute-done.14.refs_0_, bf16[128,3072]{1,0:T(8,128)(2,1)} %collective-permute-done.19.refs_1_, ...), custom_call_target="tpu_custom_call" | custom-call | flops 4831838208 | bytes 4831838 | tf_op jit(solution)/shard_map/attn_terms/pallas_call | solution.py:173
  342.6 3.9 collective-permute-done.21.refs_2_
  346.5 2.1 collective-permute-start.24
  349.6 3.6 broadcast_select_fusion.1
  353.2 12.2 %attn_terms.3 = (bf16[2,128,1536]{2,1,0:T(8,128)(2,1)}, f32[2,128,1536]{2,1,0:T(8,128)}, bf16[4,128,3072]{2,1,0:T(8,128)(2,1)}) custom-call(s32[9]{0:T(128)} %pad_add_fusion.scalars, bf16[128,3072]{1,0:T(8,128)(2,1)} %collective-permute-done.18.refs_0_, bf16[128,3072]{1,0:T(8,128)(2,1)} %collective-permute-done.23.refs_1_, ...), custom_call_target="tpu_custom_call" | custom-call | flops 4831838208 | bytes 4831838 | tf_op jit(solution)/shard_map/attn_terms/pallas_call | solution.py:173
  365.3 3.5 collective-permute-done.22
  368.9 2.2 add_convert_fusion.5
  372.0 15.1 %outer.9 = bf16[1536,3072]{1,0:T(8,128)(2,1)} custom-call(s32[4]{0:T(128)} %iota_xor_fusion.2.place.scalars, bf16[1536,1024]{1,0:T(8,128)(2,1)} %turn.3.left_ref, bf16[512,3072]{1,0:T(8,128)(2,1)} %bitcast.51, bf16[512,3072]{1,0:T(8,128)(2,1)} %bitcast.52), custom_call_target="tpu_custom_call" | custom-call | flops 9663676416 | bytes 9663676 | tf_op jit(solution)/shard_map/outer/pallas_call | solution.py:221
  387.1 4.5 %collective-permute-done.25 = bf16[1,128,1536]{2,1,0:T(8,128)(2,1)} collective-permute-done((bf16[1,128,1536]{2,1,0:T(8,128)(2,1)}, bf16[1,128,1536]{2,1,0:T(8,128)(2,1)}, u32[]{:S(2)}, u32[]{:S(2)}) %collective-permute-start.25) | collective-permute-done | bytes 393248 | tf_op jit(solution)/shard_map/ppermute | solution.py:34
  391.6 7.4 %collective-permute-done.26 = bf16[2,128,1536]{2,1,0:T(8,128)(2,1)} collective-permute-done((bf16[2,128,1536]{2,1,0:T(8,128)(2,1)}, bf16[2,128,1536]{2,1,0:T(8,128)(2,1)}, u32[]{:S(2)}, u32[]{:S(2)}) %collective-permute-start.26) | collective-permute-done | bytes 786464 | tf_op jit(solution)/shard_map/ppermute | solution.py:34
  402.2 3.3 fusion.1
  406.8 12.9 %collective-permute-done.27 = bf16[1,128,1536]{2,1,0:T(8,128)(2,1)S(1)} collective-permute-done((bf16[1,128,1536]{2,1,0:T(8,128)(2,1)S(1)}, bf16[1,128,1536]{2,1,0:T(8,128)(2,1)S(1)}, u32[]{:S(2)}, u32[]{:S(2)}) %collective-permute-start.27) | collective-permute-done | bytes 393248 | tf_op jit(solution)/shard_map/ppermute | solution.py:34
  (69 shorter events, 18.4 us)
Async XLA Ops:
  3.0 30.7 %collective-permute-start = (bf16[256,2304]{1,0:T(8,128)(2,1)}, bf16[256,2304]{1,0:T(8,128)(2,1)}, u32[]{:S(2)}, u32[]{:S(2)}) collective-permute-start(bf16[256,2304]{1,0:T(8,128)(2,1)} %slice.77), channel_id=1, source_target_pairs={{0,0},{5,1},{10,2},{15,3},{1,4},{4,5},{11,6},{14,7},{2,8},{7,9},{8... | collective-permute-start | bytes 3538952 | tf_op jit(solution)/shard_map/ppermute | solution.py:56
  13.4 28.6 %collective-permute-start.1 = (bf16[256,2304]{1,0:T(8,128)(2,1)}, bf16[256,2304]{1,0:T(8,128)(2,1)}, u32[]{:S(2)}, u32[]{:S(2)}) collective-permute-start(bf16[256,2304]{1,0:T(8,128)(2,1)} %slice.77), channel_id=1, source_target_pairs={{1,0},{4,1},{11,2},{14,3},{0,4},{5,5},{10,6},{15,7},{3,8},{6,9},{9... | collective-permute-start | bytes 3538952 | tf_op jit(solution)/shard_map/ppermute | solution.py:56
  15.3 54.7 %collective-permute-start.2 = (bf16[256,2304]{1,0:T(8,128)(2,1)}, bf16[256,2304]{1,0:T(8,128)(2,1)}, u32[]{:S(2)}, u32[]{:S(2)}) collective-permute-start(bf16[256,2304]{1,0:T(8,128)(2,1)} %slice.77), channel_id=1, source_target_pairs={{2,0},{7,1},{8,2},{13,3},{3,4},{6,5},{9,6},{12,7},{0,8},{5,9},{10,... | collective-permute-start | bytes 3538952 | tf_op jit(solution)/shard_map/ppermute | solution.py:56
  17.2 67.4 %collective-permute-start.3 = (bf16[256,2304]{1,0:T(8,128)(2,1)}, bf16[256,2304]{1,0:T(8,128)(2,1)}, u32[]{:S(2)}, u32[]{:S(2)}) collective-permute-start(bf16[256,2304]{1,0:T(8,128)(2,1)} %slice.77), channel_id=1, source_target_pairs={{3,0},{6,1},{9,2},{12,3},{2,4},{7,5},{8,6},{13,7},{1,8},{4,9},{11,... | collective-permute-start | bytes 3538952 | tf_op jit(solution)/shard_map/ppermute | solution.py:56
  27.5 6.0 %copy-start.6 = (bf16[1,256,4608]{2,1,0:T(8,128)(2,1)S(1)}, bf16[1,256,4608]{2,1,0:T(8,128)(2,1)}, u32[]{:S(2)}) copy-start(bf16[1,256,4608]{2,1,0:T(8,128)(2,1)} %param.7) | copy-start | bytes 7077892
  84.6 69.7 %collective-permute-start.4 = (bf16[128,2304]{1,0:T(8,128)(2,1)S(1)}, bf16[128,2304]{1,0:T(8,128)(2,1)S(1)}, u32[]{:S(2)}, u32[]{:S(2)}) collective-permute-start(bf16[128,2304]{1,0:T(8,128)(2,1)S(1)} %get-tuple-element.54), channel_id=1, source_target_pairs={{0,0},{5,1},{10,2},{15,3},{1,4},{4,5},{11,6},{14,7},{2,8},{7,9},{8... | collective-permute-start | bytes 1769480 | tf_op jit(solution)/shard_map/ppermute | solution.py:56
  85.3 69.0 %collective-permute-start.5 = (bf16[128,2304]{1,0:T(8,128)(2,1)S(1)}, bf16[128,2304]{1,0:T(8,128)(2,1)S(1)}, u32[]{:S(2)}, u32[]{:S(2)}) collective-permute-start(bf16[128,2304]{1,0:T(8,128)(2,1)S(1)} %get-tuple-element.54), channel_id=1, source_target_pairs={{1,0},{4,1},{11,2},{14,3},{0,4},{5,5},{10,6},{15,7},{3,8},{6,9},{9... | collective-permute-start | bytes 1769480 | tf_op jit(solution)/shard_map/ppermute | solution.py:56
  121.5 32.8 %collective-permute-start.6 = (bf16[128,2304]{1,0:T(8,128)(2,1)S(1)}, bf16[128,2304]{1,0:T(8,128)(2,1)S(1)}, u32[]{:S(2)}, u32[]{:S(2)}) collective-permute-start(bf16[128,2304]{1,0:T(8,128)(2,1)S(1)} %get-tuple-element.54), channel_id=1, source_target_pairs={{2,0},{7,1},{8,2},{13,3},{3,4},{6,5},{9,6},{12,7},{0,8},{5,9},{10,... | collective-permute-start | bytes 1769480 | tf_op jit(solution)/shard_map/ppermute | solution.py:56
  125.6 28.7 %collective-permute-start.7 = (bf16[128,2304]{1,0:T(8,128)(2,1)S(1)}, bf16[128,2304]{1,0:T(8,128)(2,1)S(1)}, u32[]{:S(2)}, u32[]{:S(2)}) collective-permute-start(bf16[128,2304]{1,0:T(8,128)(2,1)S(1)} %get-tuple-element.54), channel_id=1, source_target_pairs={{3,0},{6,1},{9,2},{12,3},{2,4},{7,5},{8,6},{13,7},{1,8},{4,9},{11,... | collective-permute-start | bytes 1769480 | tf_op jit(solution)/shard_map/ppermute | solution.py:56
  154.3 38.2 %copy-start.11 = (bf16[128,2304]{1,0:T(8,128)(2,1)}, bf16[128,2304]{1,0:T(8,128)(2,1)S(1)}, u32[]{:S(2)}) copy-start(bf16[128,2304]{1,0:T(8,128)(2,1)S(1)} %collective-permute-done.4.refs_0_) | copy-start | bytes 1769476
  154.3 38.2 %copy-start.12 = (bf16[128,2304]{1,0:T(8,128)(2,1)}, bf16[128,2304]{1,0:T(8,128)(2,1)S(1)}, u32[]{:S(2)}) copy-start(bf16[128,2304]{1,0:T(8,128)(2,1)S(1)} %collective-permute-done.5.refs_1_) | copy-start | bytes 1769476
  154.4 38.2 %copy-start.13 = (bf16[128,2304]{1,0:T(8,128)(2,1)}, bf16[128,2304]{1,0:T(8,128)(2,1)S(1)}, u32[]{:S(2)}) copy-start(bf16[128,2304]{1,0:T(8,128)(2,1)S(1)} %collective-permute-done.6.refs_2_) | copy-start | bytes 1769476
  154.4 38.2 %copy-start.14 = (bf16[128,2304]{1,0:T(8,128)(2,1)}, bf16[128,2304]{1,0:T(8,128)(2,1)S(1)}, u32[]{:S(2)}) copy-start(bf16[128,2304]{1,0:T(8,128)(2,1)S(1)} %collective-permute-done.7.refs_3_) | copy-start | bytes 1769476
  154.4 74.8 %collective-permute-start.8 = (bf16[128,2304]{1,0:T(8,128)(2,1)S(1)}, bf16[128,2304]{1,0:T(8,128)(2,1)}, u32[]{:S(2)}, u32[]{:S(2)}) collective-permute-start(bf16[128,2304]{1,0:T(8,128)(2,1)S(1)} %get-tuple-element.60), channel_id=1, source_target_pairs={{0,0},{5,1},{10,2},{15,3},{1,4},{4,5},{11,6},{14,7},{2,8},{7,9},{8... | collective-permute-start | bytes 1769480 | tf_op jit(solution)/shard_map/ppermute | solution.py:56
  155.9 73.2 %collective-permute-start.9 = (bf16[128,2304]{1,0:T(8,128)(2,1)S(1)}, bf16[128,2304]{1,0:T(8,128)(2,1)}, u32[]{:S(2)}, u32[]{:S(2)}) collective-permute-start(bf16[128,2304]{1,0:T(8,128)(2,1)S(1)} %get-tuple-element.60), channel_id=1, source_target_pairs={{1,0},{4,1},{11,2},{14,3},{0,4},{5,5},{10,6},{15,7},{3,8},{6,9},{9... | collective-permute-start | bytes 1769480 | tf_op jit(solution)/shard_map/ppermute | solution.py:56
  181.8 47.4 %collective-permute-start.10 = (bf16[128,2304]{1,0:T(8,128)(2,1)S(1)}, bf16[128,2304]{1,0:T(8,128)(2,1)}, u32[]{:S(2)}, u32[]{:S(2)}) collective-permute-start(bf16[128,2304]{1,0:T(8,128)(2,1)S(1)} %get-tuple-element.60), channel_id=1, source_target_pairs={{2,0},{7,1},{8,2},{13,3},{3,4},{6,5},{9,6},{12,7},{0,8},{5,9},{10,... | collective-permute-start | bytes 1769480 | tf_op jit(solution)/shard_map/ppermute | solution.py:56
  186.0 43.1 %collective-permute-start.11 = (bf16[128,2304]{1,0:T(8,128)(2,1)S(1)}, bf16[128,2304]{1,0:T(8,128)(2,1)}, u32[]{:S(2)}, u32[]{:S(2)}) collective-permute-start(bf16[128,2304]{1,0:T(8,128)(2,1)S(1)} %get-tuple-element.60), channel_id=1, source_target_pairs={{3,0},{6,1},{9,2},{12,3},{2,4},{7,5},{8,6},{13,7},{1,8},{4,9},{11,... | collective-permute-start | bytes 1769480 | tf_op jit(solution)/shard_map/ppermute | solution.py:56
  207.7 25.1 %copy-start = (f32[2,128,3072]{2,1,0:T(8,128)S(1)}, f32[2,128,3072]{2,1,0:T(8,128)}, u32[]{:S(2)}) copy-start(f32[2,128,3072]{2,1,0:T(8,128)} %get-tuple-element.58) | copy-start | bytes 9437188
  229.2 3.7 collective-permute-start.12
  232.9 1.2 copy-start.2
  234.0 31.6 %collective-permute-start.13 = (bf16[1,128,3072]{2,1,0:T(8,128)(2,1)S(1)}, bf16[1,128,3072]{2,1,0:T(8,128)(2,1)}, u32[]{:S(2)}, u32[]{:S(2)}) collective-permute-start(bf16[1,128,3072]{2,1,0:T(8,128)(2,1)S(1)} %add_convert_fusion.1), channel_id=1, source_target_pairs={{0,2},{1,3},{2,0},{3,1},{4,6},{5,7},{6,4},{7,5},{8,10},{9,11},{10,... | collective-permute-start | bytes 2359304 | tf_op jit(solution)/shard_map/ppermute | solution.py:34
  265.6 4.5 %collective-permute-start.15 = (bf16[2,128,3072]{2,1,0:T(8,128)(2,1)}, bf16[2,128,3072]{2,1,0:T(8,128)(2,1)}, u32[]{:S(2)}, u32[]{:S(2)}) collective-permute-start(bf16[2,128,3072]{2,1,0:T(8,128)(2,1)} %get-tuple-element.70), channel_id=1, source_target_pairs={{0,1},{1,0},{2,3},{3,2},{4,5},{5,4},{6,7},{7,6},{8,9},{9,8},{10,11... | collective-permute-start | bytes 4718600 | tf_op jit(solution)/shard_map/ppermute | solution.py:34
  265.6 4.5 %copy-start.1 = (f32[2,128,3072]{2,1,0:T(8,128)S(1)}, f32[2,128,3072]{2,1,0:T(8,128)}, u32[]{:S(2)}) copy-start(f32[2,128,3072]{2,1,0:T(8,128)} %get-tuple-element.69) | copy-start | bytes 9437188
  268.7 26.0 %collective-permute-start.14 = (bf16[128,3072]{1,0:T(8,128)(2,1)}, bf16[128,3072]{1,0:T(8,128)(2,1)}, u32[]{:S(2)}, u32[]{:S(2)}) collective-permute-start(bf16[128,3072]{1,0:T(8,128)(2,1)} %fusion.2), channel_id=1, source_target_pairs={{16,0},{17,1},{18,2},{19,3},{20,4},{21,5},{22,6},{23,7},{24,8},{25... | collective-permute-start | bytes 2359304 | tf_op jit(solution)/shard_map/ppermute | solution.py:50
  272.4 22.3 %collective-permute-start.16 = (bf16[1,128,3072]{2,1,0:T(8,128)(2,1)}, bf16[1,128,3072]{2,1,0:T(8,128)(2,1)S(1)}, u32[]{:S(2)}, u32[]{:S(2)}) collective-permute-start(bf16[1,128,3072]{2,1,0:T(8,128)(2,1)} %add_convert_fusion), channel_id=1, source_target_pairs={{0,2},{1,3},{2,0},{3,1},{4,6},{5,7},{6,4},{7,5},{8,10},{9,11},{10,... | collective-permute-start | bytes 2359304 | tf_op jit(solution)/shard_map/ppermute | solution.py:34
  294.7 3.5 copy-start.4
  298.2 29.5 %copy-start.15 = (s32[4]{0:T(128)S(1)}, s32[4]{0:T(128)}, u32[]{:S(2)}) copy-start(s32[4]{0:T(128)} %iota_xor_fusion.1.token) | copy-start | bytes 52
  298.2 22.0 %collective-permute-start.17 = (bf16[128,3072]{1,0:T(8,128)(2,1)}, bf16[128,3072]{1,0:T(8,128)(2,1)}, u32[]{:S(2)}, u32[]{:S(2)}) collective-permute-start(bf16[128,3072]{1,0:T(8,128)(2,1)} %collective-permute-done.14.refs_0_), channel_id=1, source_target_pairs={{0,2},{1,3},{2,0},{3,1},{4,6},{5,7},{6,4},{7,5},{8,10},{9,11},{10,... | collective-permute-start | bytes 2359304 | tf_op jit(solution)/shard_map/ppermute | solution.py:44
  300.5 21.9 %collective-permute-start.18 = (bf16[128,3072]{1,0:T(8,128)(2,1)}, bf16[128,3072]{1,0:T(8,128)(2,1)}, u32[]{:S(2)}, u32[]{:S(2)}) collective-permute-start(bf16[128,3072]{1,0:T(8,128)(2,1)} %fusion), channel_id=1, source_target_pairs={{16,0},{17,1},{18,2},{19,3},{20,4},{21,5},{22,6},{23,7},{24,8},{25... | collective-permute-start | bytes 2359304 | tf_op jit(solution)/shard_map/ppermute | solution.py:50
  301.8 28.6 %collective-permute-start.19 = (bf16[128,3072]{1,0:T(8,128)(2,1)}, bf16[128,3072]{1,0:T(8,128)(2,1)}, u32[]{:S(2)}, u32[]{:S(2)}) collective-permute-start(bf16[128,3072]{1,0:T(8,128)(2,1)} %collective-permute-done.14.refs_0_), channel_id=1, source_target_pairs={{0,1},{1,0},{2,3},{3,2},{4,5},{5,4},{6,7},{7,6},{8,9},{9,8},{10,11... | collective-permute-start | bytes 2359304 | tf_op jit(solution)/shard_map/ppermute | solution.py:44
  322.4 8.0 %collective-permute-start.20 = (bf16[128,3072]{1,0:T(8,128)(2,1)}, bf16[128,3072]{1,0:T(8,128)(2,1)}, u32[]{:S(2)}, u32[]{:S(2)}) collective-permute-start(bf16[128,3072]{1,0:T(8,128)(2,1)} %collective-permute-done.17.refs_2_), channel_id=1, source_target_pairs={{0,1},{1,0},{2,3},{3,2},{4,5},{5,4},{6,7},{7,6},{8,9},{9,8},{10,11... | collective-permute-start | bytes 2359304 | tf_op jit(solution)/shard_map/ppermute | solution.py:44
  324.4 22.2 %collective-permute-start.21 = (bf16[128,3072]{1,0:T(8,128)(2,1)}, bf16[128,3072]{1,0:T(8,128)(2,1)}, u32[]{:S(2)}, u32[]{:S(2)}) collective-permute-start(bf16[128,3072]{1,0:T(8,128)(2,1)} %collective-permute-done.18.refs_0_), channel_id=1, source_target_pairs={{0,2},{1,3},{2,0},{3,1},{4,6},{5,7},{6,4},{7,5},{8,10},{9,11},{10,... | collective-permute-start | bytes 2359304 | tf_op jit(solution)/shard_map/ppermute | solution.py:44
  328.3 24.9 %collective-permute-start.23 = (bf16[128,3072]{1,0:T(8,128)(2,1)}, bf16[128,3072]{1,0:T(8,128)(2,1)}, u32[]{:S(2)}, u32[]{:S(2)}) collective-permute-start(bf16[128,3072]{1,0:T(8,128)(2,1)} %collective-permute-done.18.refs_0_), channel_id=1, source_target_pairs={{0,1},{1,0},{2,3},{3,2},{4,5},{5,4},{6,7},{7,6},{8,9},{9,8},{10,11... | collective-permute-start | bytes 2359304 | tf_op jit(solution)/shard_map/ppermute | solution.py:44
  346.5 6.7 %collective-permute-start.24 = (bf16[128,3072]{1,0:T(8,128)(2,1)}, bf16[128,3072]{1,0:T(8,128)(2,1)}, u32[]{:S(2)}, u32[]{:S(2)}) collective-permute-start(bf16[128,3072]{1,0:T(8,128)(2,1)} %collective-permute-done.21.refs_2_), channel_id=1, source_target_pairs={{0,1},{1,0},{2,3},{3,2},{4,5},{5,4},{6,7},{7,6},{8,9},{9,8},{10,11... | collective-permute-start | bytes 2359304 | tf_op jit(solution)/shard_map/ppermute | solution.py:44
  348.6 20.2 %collective-permute-start.22 = (bf16[2,128,1536]{2,1,0:T(8,128)(2,1)}, bf16[2,128,1536]{2,1,0:T(8,128)(2,1)S(1)}, u32[]{:S(2)}, u32[]{:S(2)}) collective-permute-start(bf16[2,128,1536]{2,1,0:T(8,128)(2,1)} %get-tuple-element.84), channel_id=1, source_target_pairs={{0,4},{4,0},{8,12},{12,8},{1,5},{5,1},{9,13},{13,9},{2,6},{6,2},{1... | collective-permute-start | bytes 2359304 | tf_op jit(solution)/shard_map/ppermute | solution.py:34
  368.9 3.1 copy-start.9
  371.1 20.5 %collective-permute-start.25 = (bf16[1,128,1536]{2,1,0:T(8,128)(2,1)}, bf16[1,128,1536]{2,1,0:T(8,128)(2,1)}, u32[]{:S(2)}, u32[]{:S(2)}) collective-permute-start(bf16[1,128,1536]{2,1,0:T(8,128)(2,1)} %add_convert_fusion.5), channel_id=1, source_target_pairs={{0,8},{4,12},{8,0},{12,4},{1,9},{5,13},{9,1},{13,5},{2,10},{6,14},... | collective-permute-start | bytes 1179656 | tf_op jit(solution)/shard_map/ppermute | solution.py:34
  371.1 27.9 %collective-permute-start.26 = (bf16[2,128,1536]{2,1,0:T(8,128)(2,1)}, bf16[2,128,1536]{2,1,0:T(8,128)(2,1)}, u32[]{:S(2)}, u32[]{:S(2)}) collective-permute-start(bf16[2,128,1536]{2,1,0:T(8,128)(2,1)} %get-tuple-element.94), channel_id=1, source_target_pairs={{0,4},{4,0},{8,12},{12,8},{1,5},{5,1},{9,13},{13,9},{2,6},{6,2},{1... | collective-permute-start | bytes 2359304 | tf_op jit(solution)/shard_map/ppermute | solution.py:34
  372.0 30.2 %copy-start.5 = (bf16[1,128,3072]{2,1,0:T(8,128)(2,1)S(1)}, bf16[1,128,3072]{2,1,0:T(8,128)(2,1)}, u32[]{:S(2)}) copy-start(bf16[1,128,3072]{2,1,0:T(8,128)(2,1)} %copy-done.4) | copy-start | bytes 2359300
  387.1 15.1 %copy-start.3 = (bf16[2,128,3072]{2,1,0:T(8,128)(2,1)S(1)}, bf16[2,128,3072]{2,1,0:T(8,128)(2,1)}, u32[]{:S(2)}) copy-start(bf16[2,128,3072]{2,1,0:T(8,128)(2,1)} %copy-done.2) | copy-start | bytes 4718596
  400.3 19.3 %collective-permute-start.27 = (bf16[1,128,1536]{2,1,0:T(8,128)(2,1)S(1)}, bf16[1,128,1536]{2,1,0:T(8,128)(2,1)S(1)}, u32[]{:S(2)}, u32[]{:S(2)}) collective-permute-start(bf16[1,128,1536]{2,1,0:T(8,128)(2,1)S(1)} %add_convert_fusion.3), channel_id=1, source_target_pairs={{0,8},{4,12},{8,0},{12,4},{1,9},{5,13},{9,1},{13,5},{2,10},{6,14},... | collective-permute-start | bytes 1179656 | tf_op jit(solution)/shard_map/ppermute | solution.py:34
  402.2 17.5 %copy-start.10 = (bf16[2,128,1536]{2,1,0:T(8,128)(2,1)S(1)}, bf16[2,128,1536]{2,1,0:T(8,128)(2,1)}, u32[]{:S(2)}) copy-start(bf16[2,128,1536]{2,1,0:T(8,128)(2,1)} %copy-done.9) | copy-start | bytes 2359300
  405.5 14.2 %copy-start.7 = (f32[2,128,1536]{2,1,0:T(8,128)S(1)}, f32[2,128,1536]{2,1,0:T(8,128)}, u32[]{:S(2)}) copy-start(f32[2,128,1536]{2,1,0:T(8,128)} %get-tuple-element.88) | copy-start | bytes 4718596
  405.5 14.2 %copy-start.8 = (f32[2,128,1536]{2,1,0:T(8,128)S(1)}, f32[2,128,1536]{2,1,0:T(8,128)}, u32[]{:S(2)}) copy-start(f32[2,128,1536]{2,1,0:T(8,128)} %get-tuple-element.96) | copy-start | bytes 4718596
